TPU v7x, 256 devices: a whole 4x4x8 slice. The times are simulated.
256 devices in a mesh: ctx: 64 (over x_lo, y, z), tp: 4 (over x_hi, core).
Axes of the slice: x: 4 (x_hi: 2, x_lo: 2; x = x_hi * 2 + x_lo), y: 4, z: 8, core: 2. Of those that a mesh axis runs over, the one named last changes fastest.
Arguments:
- queries: bfloat16 [8192, 1024], P('ctx', 'tp'), may hold values from -18 to 18
- keys: bfloat16 [8192, 1024], P('ctx', 'tp'), may hold values from -18 to 18
- values: bfloat16 [8192, 1024], P('ctx', 'tp'), may hold values from -6 to 6
- out_grad: bfloat16 [8192, 2048], P('ctx'), may hold values from -16 to 16
- w_out: bfloat16 [1024, 2048], P('tp'), may hold values from -0.1875 to 0.1875
- frame_index: int32 [8192], replicated, may hold values from 0 to 31, as said below
- group_order: int32 [128], replicated, may hold values from 0 to 127, as said below
Outputs:
- grad_queries: bfloat16 [8192, 1024], P('ctx', 'tp')
- grad_keys: bfloat16 [8192, 1024], P('ctx', 'tp')
- grad_values: bfloat16 [8192, 1024], P('ctx', 'tp')
- grad_w_out: float32 [1024, 2048], P('tp', 'ctx')
Inputs may be any that keep to these rules, and one draw needn't show every extreme that they name: `frame_index`: nondecreasing along the sequence, every frame holds one or more tokens. `group_order`: each group number appears once.
All inputs are finite; a program needn't handle non-finite values.
Results may differ from a plain program's by a relative error of at most 0.03.
Values may be sent and summed in bfloat16 or wider, within the bound.
A program may use at most 128 MiB of HBM per device.

v0:
```python
import math

import jax
import jax.numpy as jnp
from jax import lax
from jax.sharding import PartitionSpec as P

HD = 128


masked_score = -1e30


def head_scores(query_block, key_block, query_frames, key_frames):
    scores = jnp.einsum(
        "qhd,khd->hqk", query_block, key_block, preferred_element_type=jnp.float32
    ) * HD ** (-0.5)
    allowed = key_frames[None, :] <= query_frames[:, None]
    return (jnp.where(allowed[None], scores, masked_score), allowed)


def forward_update(running, query_heads, query_frames, key_block, value_block, key_frames):
    row_max, row_total, summed = running
    scores, allowed = head_scores(query_heads, key_block, query_frames, key_frames)
    new_max = jnp.maximum(row_max, jnp.max(scores, axis=-1))
    weights = jnp.where(allowed[None], jnp.exp(scores - new_max[:, :, None]), 0.0)
    factor = jnp.exp(row_max - new_max)
    row_total = row_total * factor + jnp.sum(weights, axis=-1)
    product = jnp.einsum(
        "hqk,khd->qhd",
        weights.astype(jnp.bfloat16),
        value_block,
        preferred_element_type=jnp.float32,
    )
    summed = summed * jnp.transpose(factor)[:, :, None] + product
    return (new_max, row_total, summed)


def gradient_tile(
    query_block,
    grad_block,
    log_block,
    delta_block,
    query_frames,
    key_block,
    value_block,
    key_frames,
):
    scores, allowed = head_scores(query_block, key_block, query_frames, key_frames)
    probs = jnp.exp(scores - jnp.transpose(log_block)[:, :, None])
    grad_probs = jnp.einsum(
        "qhd,khd->hqk", grad_block, value_block, preferred_element_type=jnp.float32
    )
    grad_scores = (probs * (grad_probs - jnp.transpose(delta_block)[:, :, None])).astype(
        jnp.bfloat16
    )
    return (probs.astype(jnp.bfloat16), grad_scores)


def shards(queries, keys, values, out_grad, w_out, frame_index, group_order):
    local_rows = queries.shape[0]
    width_dev = queries.shape[1]
    heads_dev = width_dev // HD
    group_rows = local_rows // 2
    ctx_size = lax.axis_size("ctx")
    all_rows = local_rows * ctx_size
    my_index = lax.axis_index("ctx")
    block_rows = local_rows * math.gcd(ctx_size, 8)
    block_count = all_rows // block_rows

    def frames_of(first_row, length):
        stored = first_row + jnp.arange(length, dtype=jnp.int32)
        position = group_order[stored // group_rows] * group_rows + stored % group_rows
        return frame_index[position]

    def to_blocks(array):
        return array.reshape((block_count, block_rows) + array.shape[1:])

    my_frames = frames_of(my_index * local_rows, local_rows)
    query_heads = queries.reshape(local_rows, heads_dev, HD)
    d_attn = lax.dot_general(
        out_grad, w_out, (((1,), (1,)), ((), ())), preferred_element_type=jnp.float32
    ).astype(jnp.bfloat16)
    grad_heads = d_attn.reshape(local_rows, heads_dev, HD)
    start_state = (
        jnp.full((heads_dev, local_rows), masked_score, jnp.float32),
        jnp.zeros((heads_dev, local_rows), jnp.float32),
        jnp.zeros((local_rows, heads_dev, HD), jnp.float32),
    )

    def forward_piece(running, key_block, value_block, key_frames):
        return forward_update(running, query_heads, my_frames, key_block, value_block, key_frames)

    whole_keys, whole_values = (
        lax.all_gather(keys, "ctx", axis=0, tiled=True),
        lax.all_gather(values, "ctx", axis=0, tiled=True),
    )
    key_blocks = to_blocks(whole_keys.reshape(all_rows, heads_dev, HD))
    value_blocks = to_blocks(whole_values.reshape(all_rows, heads_dev, HD))
    key_frame_blocks = to_blocks(frames_of(0, all_rows))

    def forward_step(running, block_data):
        return (forward_piece(running, block_data[0], block_data[1], block_data[2]), ())

    (row_max, row_total, summed), unused = lax.scan(
        forward_step, start_state, (key_blocks, value_blocks, key_frame_blocks)
    )
    attended = (
        (summed / jnp.transpose(row_total)[:, :, None])
        .reshape(local_rows, width_dev)
        .astype(jnp.bfloat16)
    )
    log_rows = jnp.transpose(row_max + jnp.log(row_total))
    delta_rows = jnp.sum(
        (d_attn.astype(jnp.float32) * attended.astype(jnp.float32)).reshape(
            local_rows, heads_dev, HD
        ),
        axis=-1,
    )
    weight_rows = lax.psum_scatter(
        lax.dot_general(
            out_grad, attended, (((0,), (0,)), ((), ())), preferred_element_type=jnp.float32
        ),
        "ctx",
        scatter_dimension=0,
        tiled=True,
    )
    grad_w_out = jnp.transpose(weight_rows)
    zero_rows = jnp.zeros((local_rows, heads_dev, HD), jnp.float32)

    def scan_step(query_total, block_data):
        key_block, value_block, key_frames = block_data
        probs_low, grad_scores = gradient_tile(
            query_heads,
            grad_heads,
            log_rows,
            delta_rows,
            my_frames,
            key_block,
            value_block,
            key_frames,
        )
        new_total = query_total + jnp.einsum(
            "hqk,khd->qhd", grad_scores, key_block, preferred_element_type=jnp.float32
        )
        key_term = jnp.einsum(
            "hqk,qhd->khd", grad_scores, query_heads, preferred_element_type=jnp.float32
        )
        value_term = jnp.einsum(
            "hqk,qhd->khd", probs_low, grad_heads, preferred_element_type=jnp.float32
        )
        return (new_total, (key_term, value_term))

    query_sum, key_parts = lax.scan(
        scan_step, zero_rows, (key_blocks, value_blocks, key_frame_blocks)
    )
    key_sum, value_sum = (
        lax.psum_scatter(
            key_parts[0].reshape(all_rows, width_dev), "ctx", scatter_dimension=0, tiled=True
        ),
        lax.psum_scatter(
            key_parts[1].reshape(all_rows, width_dev), "ctx", scatter_dimension=0, tiled=True
        ),
    )
    score_scale = HD ** (-0.5)
    grad_queries = (query_sum.reshape(local_rows, width_dev) * score_scale).astype(jnp.bfloat16)
    grad_keys = (key_sum * score_scale).astype(jnp.bfloat16)
    grad_values = value_sum.astype(jnp.bfloat16)
    return (grad_queries, grad_keys, grad_values, grad_w_out)


def solution(mesh):
    placed = (
        P("ctx", "tp"),
        P("ctx", "tp"),
        P("ctx", "tp"),
        P("ctx", None),
        P("tp", None),
        P(),
        P(),
    )
    return jax.shard_map(
        shards,
        mesh=mesh,
        in_specs=placed,
        out_specs=(P("ctx", "tp"), P("ctx", "tp"), P("ctx", "tp"), P("tp", "ctx")),
        check_vma=False,
    )
```

profile of v0, /device:TPU:4, one launch (start us, length us, event | category | flops | bytes accessed | tf_op | source)
XLA Modules:
  0.0 1713.1 jit_solution(16856811326503347044)
XLA Ops:
  8.8 1.6 gather_fusion.2
  10.5 48.9 %gather_fusion = s32[8192]{0:T(1024)S(1)} fusion(s32[128]{0:T(128)S(1)} %copy-done.2, s32[8192]{0:T(1024)S(1)} %broadcast_clamp_fusion.1), kind=kCustom, calls=%fused_computation | custom fusion | bytes 98304 | tf_op jit(solution)/shard_map/gather | solution.py:73
  60.7 45.5 %gather_fusion.1 = s32[8192]{0:T(1024)S(1)} fusion(s32[8192]{0:T(1024)S(1)} %copy-done.3, s32[8192]{0:T(1024)S(1)} %broadcast_clamp_fusion), kind=kCustom, calls=%fused_computation.1 | custom fusion | bytes 98304 | tf_op jit(solution)/shard_map/gather | solution.py:74
  106.5 209.9 %all-gather.3.cloned.1.call-done = bf16[8192,256]{1,0:T(8,128)(2,1)} async-done(((bf16[128,256]{1,0:T(8,128)(2,1)}), bf16[8192,256]{1,0:T(8,128)(2,1)}) %all-gather.3.cloned.1.call-update) | async-done | bytes 4194320 | tf_op jit(solution)/shard_map/all_gather | solution.py:95
  316.4 7.0 reshape.313
  323.3 5.0 copy.49
  328.3 291.5 %all-gather.5.cloned.1.call-done = bf16[8192,256]{1,0:T(8,128)(2,1)} async-done(((bf16[128,256]{1,0:T(8,128)(2,1)}), bf16[8192,256]{1,0:T(8,128)(2,1)}) %all-gather.5.cloned.1.call-update) | async-done | bytes 4194320 | tf_op jit(solution)/shard_map/all_gather | solution.py:96
  619.7 7.0 reshape.314
  626.7 32.9 %while.30 = (s32[]{:T(128)}, f32[2,128]{1,0:T(2,128)S(1)}, f32[2,128]{1,0:T(2,128)S(1)}, f32[128,2,128]{0,2,1:T(8,128)S(1)}, s32[8,1024]{1,0:T(8,128)S(1)}, /*in...) while((s32[]{:T(128)}, f32[2,128]{1,0:T(2,128)S(1)}, ...), condition=%wide.region_3.4_spmd.clone, body=%wide.region_0.3_spmd.clone.sunk | while | flops 136807936 | bytes 7172749 | solution.py:105
  626.9 1.4 constant_dynamic-slice_fusion.9
  631.1 1.4 constant_dynamic-slice_fusion.9
  635.2 1.4 constant_dynamic-slice_fusion.9
  639.3 1.4 constant_dynamic-slice_fusion.9
  643.4 1.4 constant_dynamic-slice_fusion.9
  651.6 1.4 constant_dynamic-slice_fusion.9
  655.8 1.4 constant_dynamic-slice_fusion.9
  660.7 66.3 %while.31 = (s32[]{:T(128)}, f32[128,2,128]{0,2,1:T(8,128)S(1)}, f32[8,1024,2,128]{3,2,1,0:T(2,128)}, f32[8,1024,2,128]{3,2,1,0:T(2,128)}, bf16[8,1024,2,128]{3,...) while((s32[]{:T(128)}, f32[128,2,128]{0,2,1:T(8,128)S(1)}, ...), condition=%wide.region_6.7_spmd.clone, body=%wide.region_5.6_spmd.clone.sunk | while | flops 337575936 | bytes 14432939 | solution.py:154
  660.9 1.4 constant_dynamic-slice_fusion.11
  662.3 1.4 fusion.87
  666.1 2.9 copy_dynamic-update-slice_fusion.3
  669.2 1.4 constant_dynamic-slice_fusion.11
  670.6 1.4 fusion.87
  674.3 3.0 copy_dynamic-update-slice_fusion.3
  677.5 1.4 constant_dynamic-slice_fusion.11
  678.9 1.4 fusion.87
  682.6 2.9 copy_dynamic-update-slice_fusion.3
  687.2 1.4 fusion.87
  689.2 1.4 fusion.89
  691.0 2.9 copy_dynamic-update-slice_fusion.3
  695.5 1.4 fusion.87
  699.2 2.9 copy_dynamic-update-slice_fusion.3
  702.4 1.4 constant_dynamic-slice_fusion.11
  703.8 1.4 fusion.87
  707.5 2.9 copy_dynamic-update-slice_fusion.3
  710.7 1.4 constant_dynamic-slice_fusion.11
  712.1 1.4 fusion.87
  715.8 2.9 copy_dynamic-update-slice_fusion.3
  720.4 1.4 fusion.87
  724.1 2.9 copy_dynamic-update-slice_fusion.3
  727.0 7.1 copy.89
  734.2 7.2 copy.90
  741.5 1.5 convolution_bitcast_fusion.4
  743.0 1.9 copy.69
  745.7 318.0 %reduce-scatter.8.cloned.1.call-done = f32[128,256]{1,0:T(8,128)} async-done(((f32[8192,256]{1,0:T(8,128)}), f32[128,256]{1,0:T(8,128)}) %reduce-scatter.8.cloned.1.call-update) | async-done | bytes 131088 | tf_op jit(solution)/shard_map/reduce_scatter | solution.py:161
  1063.7 1.5 convert_element_type.44
  1065.3 327.0 %reduce-scatter.6.cloned.1.call-done = f32[128,256]{1,0:T(8,128)} async-done(((f32[8192,256]{1,0:T(8,128)}), f32[128,256]{1,0:T(8,128)}) %reduce-scatter.6.cloned.1.call-update) | async-done | bytes 131088 | tf_op jit(solution)/shard_map/reduce_scatter | solution.py:158
  1392.3 1.5 multiply_convert_fusion
  1393.8 312.8 %reduce-scatter.10.cloned.1.call-done = f32[32,256]{1,0:T(8,128)} async-done(((f32[2048,256]{1,0:T(8,128)}), f32[32,256]{1,0:T(8,128)}) %reduce-scatter.10.cloned.1.call-update) | async-done | bytes 32784
  (174 shorter events, 50.1 us)
Async XLA Ops:
  7.2 652.6 %copy-start = (bf16[256,2048]{1,0:T(8,128)(2,1)S(1)}, bf16[256,2048]{1,0:T(8,128)(2,1)}, u32[]{:S(2)}) copy-start(bf16[256,2048]{1,0:T(8,128)(2,1)} %param.15) | copy-start | bytes 3145732
  7.2 3.3 copy-start.2
  7.2 309.2 %all-gather.3.cloned.1.call-start = ((), (), s32[]{:S(2)}) async-start(), calls=%async_computation.3 | async-start | bytes 4259840 | tf_op jit(solution)/shard_map/all_gather | solution.py:95
  7.9 611.8 %all-gather.5.cloned.1.call-start = ((), (), s32[]{:S(2)}) async-start(), calls=%async_computation.4 | async-start | bytes 4259840 | tf_op jit(solution)/shard_map/all_gather | solution.py:96
  8.7 1055.0 %reduce-scatter.8.cloned.1.call-start = ((), (), s32[]{:S(2)}) async-start(), calls=%async_computation.6 | async-start | bytes 8519680 | tf_op jit(solution)/shard_map/reduce_scatter | solution.py:161
  10.5 48.9 %copy-start.3 = (s32[8192]{0:T(1024)S(1)}, s32[8192]{0:T(1024)}, u32[]{:S(2)}) copy-start(s32[8192]{0:T(1024)} %param.16) | copy-start | bytes 98308
  60.7 45.6 %copy-start.5 = (bf16[128,256]{1,0:T(8,128)(2,1)S(1)}, bf16[128,256]{1,0:T(8,128)(2,1)}, u32[]{:S(2)}) copy-start(bf16[128,256]{1,0:T(8,128)(2,1)} %param.11) | copy-start | bytes 196612
  626.7 33.1 %copy-start.4 = (bf16[128,2048]{1,0:T(8,128)(2,1)S(1)}, bf16[128,2048]{1,0:T(8,128)(2,1)}, u32[]{:S(2)}) copy-start(bf16[128,2048]{1,0:T(8,128)(2,1)} %param.14) | copy-start | bytes 1572868
  734.2 658.1 %reduce-scatter.6.cloned.1.call-start = ((), (), s32[]{:S(2)}) async-start(), calls=%async_computation.5 | async-start | bytes 8519680 | tf_op jit(solution)/shard_map/reduce_scatter | solution.py:158
  741.4 965.2 %copy-start.1 = (bf16[256,2048]{1,0:T(8,128)(2,1)S(1)}, bf16[256,2048]{1,0:T(8,128)(2,1)}, u32[]{:S(2)}) copy-start(bf16[256,2048]{1,0:T(8,128)(2,1)} %param.15) | copy-start | bytes 3145732
  741.4 965.2 %reduce-scatter.10.cloned.1.call-start = ((), (), s32[]{:S(2)}) async-start(), calls=%async_computation.7 | async-start | bytes 2129920
Sparse Core Ops, SparseCore 0:
  9.8 306.4 all-gather.2
  318.1 301.5 all-gather.4
  734.3 329.3 reduce-scatter.7
  1066.1 326.1 reduce-scatter.5
  1395.2 311.3 reduce-scatter.9
where the time goes:
time: 1720 us; the launch traced here: 1710 us
  waiting for transfers between devices  1460 us (85%)
  local copies, waits for them, and re-layouts  183 us (11%)
  matrix products  45.5 us (3%)
    reduce_scatter x1, waiting for transfers between devices, shards(): lax.psum_scatter(key_parts[0].reshape(all_rows, width_dev), 'ctx', scatte...  327 us
    reduce_scatter x1, waiting for transfers between devices, shards(): lax.psum_scatter(key_parts[1].reshape(all_rows, width_dev), 'ctx', scatte...  318 us
    unnamed x6, waiting for transfers between devices  314 us
    all_gather x1, waiting for transfers between devices, shards(): lax.all_gather(values, 'ctx', axis=0, tiled=True)  291 us
    all_gather x1, waiting for transfers between devices, shards(): lax.all_gather(keys, 'ctx', axis=0, tiled=True)  210 us
    gather x2, local copies, waits for them, and re-layouts, frames_of(): group_order[stored // group_rows] * group_rows + stored % group_rows  50.5 us
    gather x2, local copies, waits for them, and re-layouts, frames_of(): return frame_index[position]  46.7 us
  transfers between devices with their start and end apart: 5, of which 5 were waited for; matrix products, arithmetic and copies ran while one was open for 7% of the time, Pallas kernels for 0%

commit v1 on v0

v1 whole, which is shorter than its diff:
```python
import functools
import math

import jax
import jax.numpy as jnp
from jax import lax
from jax.experimental import pallas as pl
from jax.experimental.pallas import tpu as pltpu
from jax.sharding import PartitionSpec as P

HD = 128
T = 128
B = 2 * T
MASKED = -1e30
FLOOR = -1e29
SCALE = HD**-0.5
EXP2_SCALE = SCALE * math.log2(math.e)
F32 = jnp.float32
BF16 = jnp.bfloat16
NT = (((1,), (1,)), ((), ()))
TN = (((0,), (0,)), ((), ()))
MESH = pl.DeviceIdType.MESH


def dot(a, b):
    return jnp.dot(a, b, preferred_element_type=F32)


def dot_general(a, b, dims):
    return lax.dot_general(a, b, dims, preferred_element_type=F32)


def kernel(
    ny,
    nz,
    q_hbm,
    k_hbm,
    v_hbm,
    og_hbm,
    w_hbm,
    fi_hbm,
    go_hbm,
    gq_ref,
    gk_ref,
    gv_ref,
    gw_ref,
    q_in,
    k_in,
    v_in,
    og_in,
    w_in,
    fi_in,
    go_in,
    da,
    kv,
    qd,
    frames,
    kf,
    qf,
    wts,
    dps,
    obuf,
    mst,
    lst,
    dst,
    stats,
    cst,
    dlt,
    osend,
    orecv,
    att,
    ogb,
    gsend,
    grecv,
    acc_k,
    acc_v,
    acc_q,
    rsk_out,
    rsk_in,
    rsv_out,
    rsv_in,
    qsend,
    qrecv,
    fin_out,
    fin_in,
    in_sem,
    xs_s,
    xs_r,
    z_s,
    z_r,
    y_s,
    y_r,
    og_s,
    og_r,
    st_s,
    st_r,
    o_s,
    o_r,
    att_s,
    att_r,
    g_s,
    g_r,
    rs_s,
    rs_r,
    dq_s,
    dq_r,
    fin_s,
    fin_r,
):
    half = nz // 2
    me = lax.axis_index("ctx")
    x = me // (ny * nz)
    y = lax.rem(me // nz, ny)
    z = lax.rem(me, nz)
    px = 1 - x
    cols = og_in.shape[1] // (2 * ny)
    zcols = cols // nz

    def at(xx, yy, zz):
        return xx * (ny * nz) + yy * nz + zz

    partner = at(px, y, z)
    right = at(x, y, lax.rem(z + 1, nz))
    left = at(x, y, lax.rem(z + nz - 1, nz))
    ypos = [lax.rem(y + k, ny) for k in range(ny)]
    ypeer = [at(x, ypos[k], z) for k in range(ny)]
    ydiag = [at(px, ypos[k], z) for k in range(ny)]
    zpos = [lax.rem(z + k, nz) for k in range(nz)]
    zpeer = [at(x, y, zpos[k]) for k in range(nz)]

    started = []

    def send(src, dst_ref, s_sem, r_sem, device):
        copy = pltpu.make_async_remote_copy(
            src_ref=src,
            dst_ref=dst_ref,
            send_sem=s_sem,
            recv_sem=r_sem,
            device_id={"ctx": device},
            device_id_type=MESH,
        )
        copy.start()
        started.append(copy)

    def arrived(dst_ref, s_sem, r_sem, device):
        pltpu.make_async_remote_copy(
            src_ref=dst_ref,
            dst_ref=dst_ref,
            send_sem=s_sem,
            recv_sem=r_sem,
            device_id={"ctx": device},
            device_id_type=MESH,
        ).wait_recv()

    loads = [
        pltpu.make_async_copy(src, to, in_sem.at[i])
        for i, (src, to) in enumerate(
            [
                (og_hbm, og_in),
                (w_hbm, w_in),
                (k_hbm, k_in),
                (v_hbm, v_in),
                (q_hbm, q_in),
                (fi_hbm, fi_in),
                (go_hbm, go_in),
            ]
        )
    ]
    for load in loads:
        load.start()
    barrier = pltpu.get_barrier_semaphore()
    peers = [partner] + ypeer[1:] + ydiag[1:] + zpeer[1:]
    for peer in peers:
        pl.semaphore_signal(barrier, inc=1, device_id={"ctx": peer}, device_id_type=MESH)
    for load in loads:
        load.wait()

    own_lanes = pl.ds(pl.multiple_of(x * HD, HD), HD)
    other_lanes = pl.ds(pl.multiple_of(px * HD, HD), HD)

    da[...] = dot_general(og_in[...], w_in[...], NT).astype(BF16)
    kv[0, 0, 0] = k_in[:, own_lanes]
    kv[0, 0, 1] = v_in[:, own_lanes]
    qd[y, 0, 0] = q_in[:, own_lanes]
    qd[y, 0, 1] = da[:, own_lanes]
    pl.semaphore_wait(barrier, len(peers))

    swap_from = [k_in, v_in, q_in, da]

    def swap_to(i):
        return kv.at[0, 1, i] if i < 2 else qd.at[y, 1, i - 2]

    for i in range(4):
        send(swap_from[i].at[:, other_lanes], swap_to(i), xs_s.at[i], xs_r.at[i], partner)

    def swapped(i):
        arrived(swap_to(i), xs_s.at[i], xs_r.at[i], partner)

    def left_slot(s):
        return s if s < half else nz - 1

    def right_slot(s):
        return half - 1 + s if s < half else nz - 1

    def z_send_right(s, c):
        source = 0 if s == 1 else left_slot(s - 1)
        slot = left_slot(s)
        send(kv.at[source, c], kv.at[slot, c], z_s.at[0, s - 1, c], z_r.at[slot, c], right)

    def z_send_left(s, c):
        source = 0 if s == 1 else right_slot(s - 1)
        slot = right_slot(s)
        send(kv.at[source, c], kv.at[slot, c], z_s.at[1, s - 1, c], z_r.at[slot, c], left)

    def z_arrived(slot, c):
        arrived(kv.at[slot, c], z_s.at[0, 0, 0], z_r.at[slot, c], left)

    def y_send(c):
        for k in range(1, ny):
            r = ny - k
            send(qd.at[y, c], qd.at[y, c], y_s.at[k, c], y_r.at[r, c], ypeer[k])

    z_send_right(1, 0)
    z_send_left(1, 0)
    y_send(0)

    go = go_in[...]
    fi = fi_in[...].astype(F32)
    pairs, lanes = fi.shape
    groups = go.shape[1]
    half_lanes = lanes // 2
    lane = lax.broadcasted_iota(jnp.int32, (pairs, lanes), 1)
    low = jnp.where(lane < half_lanes, fi, 0.0)
    high = jnp.where(lane >= half_lanes, fi, 0.0)
    low_up = jnp.concatenate([low[:, half_lanes:], low[:, :half_lanes]], axis=1)
    high_down = jnp.concatenate([high[:, half_lanes:], high[:, :half_lanes]], axis=1)
    row = lax.broadcasted_iota(jnp.int32, (pairs, groups), 0)
    holds = [(go == 2 * row + p).astype(F32).astype(BF16) for p in range(2)]
    group_id = lax.broadcasted_iota(jnp.int32, (groups, pairs), 0)
    pair_id = lax.broadcasted_iota(jnp.int32, (groups, pairs), 1)
    picks = [(group_id == 2 * pair_id + e).astype(F32).astype(BF16) for e in range(2)]
    total = jnp.zeros((pairs, lanes), F32)
    for p in range(2):
        for e in range(2):
            part = ((low, low_up), (high_down, high))[p][e]
            total += dot_general(dot(holds[p], picks[e]).astype(BF16), part.astype(BF16), TN)
    frames[...] = total
    across = jnp.transpose(total)
    device_lane = lax.broadcasted_iota(jnp.int32, (lanes, pairs), 1)
    distance = (
        [0] + [nz - s for s in range(1, half)] + [s for s in range(1, half)] + [half]
    )
    for slot in range(nz):
        for c in range(2):
            source = at(x if c == 0 else px, y, zpos[distance[slot]])
            column = jnp.sum(jnp.where(device_lane == source, across, 0.0), axis=1, keepdims=True)
            kf[slot, pl.ds(c * T, T), :] = jnp.broadcast_to(column, (T, lanes))
    for b in range(ny):
        qf[pl.ds(b, 1), pl.ds(0, T)] = frames[pl.ds(at(x, b, z), 1), :]
        qf[pl.ds(b, 1), pl.ds(T, T)] = frames[pl.ds(at(px, b, z), 1), :]

    swapped(0)
    swapped(1)
    z_send_right(1, 1)
    z_send_left(1, 1)
    swapped(2)
    swapped(3)
    y_send(1)

    def og_lanes(xx, yy):
        return pl.ds(pl.multiple_of((xx * ny + yy) * cols, cols), cols)

    og_targets = [(x, k, ypeer[k]) for k in range(1, ny)] + [(px, k, ydiag[k]) for k in range(ny)]

    def og_send():
        ogb[y, x] = og_in[:, og_lanes(x, y)]
        for i, (xx, k, device) in enumerate(og_targets):
            side = 0 if i < ny - 1 else 1
            r = (ny - k) % ny
            send(
                og_in.at[:, og_lanes(xx, ypos[k])],
                ogb.at[y, x],
                og_s.at[i],
                og_r.at[side, r],
                device,
            )

    def forward(slot):
        kb = kv[slot, :, 0].reshape(B, HD)
        vb = kv[slot, :, 1].reshape(B, HD)
        v_t = jnp.transpose(vb)
        key_frames = jnp.concatenate([kf[slot], kf[slot]], axis=1)

        def body(b, carry):
            scores = dot_general(kb, qd[b, :, 0].reshape(B, HD), NT)
            grads = dot_general(vb, qd[b, :, 1].reshape(B, HD), NT)
            scores = jnp.where(key_frames <= qf[pl.ds(b, 1), :], scores, MASKED)
            top = jnp.maximum(jnp.max(scores, axis=0, keepdims=True), FLOOR)
            weights = jnp.exp2((scores - top) * EXP2_SCALE)
            wts[slot, b] = weights
            dps[slot, b] = grads
            mst[slot, pl.ds(b, 1), :] = top
            lst[slot, pl.ds(b, 1), :] = jnp.sum(weights, axis=0, keepdims=True)
            dst[slot, pl.ds(b, 1), :] = jnp.sum(weights * grads, axis=0, keepdims=True)
            obuf[slot, b] = dot(v_t, weights.astype(BF16))
            return carry

        lax.fori_loop(0, ny, body, 0)

    def relay(s, c):
        z_arrived(left_slot(s), c)
        if s + 1 < half or (s + 1 == half and c == 0):
            z_send_right(s + 1, c)
        z_arrived(right_slot(s), c)
        if s + 1 < half or (s + 1 == half and c == 1):
            z_send_left(s + 1, c)

    relay(1, 0)
    relay(1, 1)
    for c in range(2):
        for k in range(1, ny):
            arrived(qd.at[ypos[k], c], y_s.at[k, c], y_r.at[k, c], ypeer[k])
    og_send()
    forward(0)
    for s in range(1, half):
        if s + 1 < half:
            forward(left_slot(s))
            relay(s + 1, 0)
            forward(right_slot(s))
            relay(s + 1, 1)
        else:
            forward(left_slot(s))
            forward(right_slot(s))
    z_arrived(nz - 1, 0)
    z_arrived(nz - 1, 1)
    forward(nz - 1)

    tops = mst[...]
    own_top = jnp.max(tops, axis=0)
    shares = jnp.exp2((tops - own_top[None]) * EXP2_SCALE)
    stats[y, 0] = own_top
    stats[y, 1] = jnp.sum(shares * lst[...], axis=0)
    stats[y, 2] = jnp.sum(shares * dst[...], axis=0)
    for k in range(1, ny):
        send(stats.at[y], stats.at[y], st_s.at[k], st_r.at[ny - k], ypeer[k])
    for k in range(1, ny):
        arrived(stats.at[ypos[k]], st_s.at[k], st_r.at[k], ypeer[k])
    all_top = stats[0, 0]
    for b in range(1, ny):
        all_top = jnp.maximum(all_top, stats[b, 0])
    row_total = jnp.zeros_like(all_top)
    delta = jnp.zeros_like(all_top)
    for b in range(ny):
        share = jnp.exp2((stats[b, 0] - all_top) * EXP2_SCALE)
        row_total += share * stats[b, 1]
        delta += share * stats[b, 2]
    inverse = 1.0 / row_total
    dlt[...] = delta * inverse
    cst[...] = jnp.exp2((tops - all_top[None]) * EXP2_SCALE) * inverse[None]

    def attended_part(b, carry):
        part = obuf[0, b] * cst[0, pl.ds(b, 1), :]
        for slot in range(1, nz):
            part += obuf[slot, b] * cst[slot, pl.ds(b, 1), :]
        osend[b] = part.astype(BF16)
        return carry

    lax.fori_loop(0, ny, attended_part, 0)
    for k in range(1, ny):
        send(osend.at[ypos[k]], orecv.at[ny - k], o_s.at[k], o_r.at[ny - k], ypeer[k])

    acc_q[...] = jnp.zeros_like(acc_q)

    def backward(slot):
        k_t = jnp.transpose(kv[slot, :, 0].reshape(B, HD))
        acc_k[...] = jnp.zeros_like(acc_k)
        acc_v[...] = jnp.zeros_like(acc_v)

        def body(b, carry):
            probs = wts[slot, b] * cst[slot, pl.ds(b, 1), :]
            grad_scores = (probs * (dps[slot, b] - dlt[pl.ds(b, 1), :])).astype(BF16)
            acc_v[...] += dot(probs.astype(BF16), qd[b, :, 1].reshape(B, HD))
            acc_k[...] += dot(grad_scores, qd[b, :, 0].reshape(B, HD))
            acc_q[b] += dot(k_t, grad_scores)
            return carry

        lax.fori_loop(0, ny, body, 0)

    def reduce_arrived(way, step, c):
        i = step - 1
        for t, to in enumerate((rsv_in, rsk_in)):
            arrived(to.at[way, i, c], rs_s.at[t, way, i, c], rs_r.at[t, way, i, c], left)
        return rsk_in[way, i, c].astype(F32), rsv_in[way, i, c]

    def reduce_send(way, step, c, arrival):
        part_k = acc_k[pl.ds(c * T, T), :]
        part_v = acc_v[pl.ds(c * T, T), :]
        if arrival:
            more_k, more_v = reduce_arrived(way, step - 1, c)
            part_k += more_k
            part_v += more_v
        i = step - 1
        rsk_out[way, i, c] = part_k.astype(BF16)
        rsv_out[way, i, c] = part_v
        device = right if way == 0 else left
        for t, (src, to) in enumerate(((rsv_out, rsv_in), (rsk_out, rsk_in))):
            send(src.at[way, i, c], to.at[way, i, c], rs_s.at[t, way, i, c], rs_r.at[t, way, i, c], device)

    backward(nz - 1)
    reduce_send(0, 1, 0, False)
    reduce_send(1, 1, 1, False)

    for k in range(1, ny):
        arrived(orecv.at[k], o_s.at[k], o_r.at[k], ypeer[k])
    rows_att = osend[y].astype(F32)
    for k in range(1, ny):
        rows_att += orecv[k].astype(F32)
    att[x, y] = rows_att.astype(BF16)
    for i, (xx, k, device) in enumerate(og_targets):
        side = 0 if i < ny - 1 else 1
        send(att.at[x, y], att.at[x, y], att_s.at[i], att_r.at[side, (ny - k) % ny], device)

    def reduce_step(step):
        d = half + 1 - step
        backward(right_slot(d))
        for c in range(2):
            reduce_send(0, step, c, step > 2 or c == 0)
        backward(left_slot(d))
        for c in range(2):
            reduce_send(1, step, c, step > 2 or c == 1)

    reduce_step(2)

    for i, (xx, k, device) in enumerate(og_targets):
        side = 0 if i < ny - 1 else 1
        source_x = x if side == 0 else px
        arrived(ogb.at[ypos[k], source_x], og_s.at[i], og_r.at[side, k], device)
        arrived(att.at[source_x, ypos[k]], att_s.at[i], att_r.at[side, k], device)
    for h in range(2):
        part = jnp.zeros((HD, cols), F32)
        for b in range(ny):
            for c in range(2):
                part += dot(att[h, b, :, pl.ds(c * T, T)], ogb[b, h ^ c])
        gsend[:, :, pl.ds(h * HD, HD)] = jnp.transpose(part).reshape(nz, zcols, HD)
    for k in range(1, nz):
        send(gsend.at[zpos[k]], grecv.at[nz - k], g_s.at[k], g_r.at[nz - k], zpeer[k])

    for step in range(3, half + 1):
        reduce_step(step)
    backward(0)

    for b in range(ny):
        qsend[b] = acc_q[b].astype(BF16)
    for k in range(1, ny):
        send(qsend.at[ypos[k]], qrecv.at[ny - k], dq_s.at[k], dq_r.at[ny - k], ypeer[k])

    for k in range(1, nz):
        arrived(grecv.at[k], g_s.at[k], g_r.at[k], zpeer[k])
    weight_rows = gsend[z]
    for k in range(1, nz):
        weight_rows += grecv[k]
    gw_ref[...] = jnp.transpose(weight_rows)

    for c in (1, 0):
        part_k = acc_k[pl.ds(c * T, T), :]
        part_v = acc_v[pl.ds(c * T, T), :]
        for way in range(2):
            more_k, more_v = reduce_arrived(way, half, c)
            part_k += more_k
            part_v += more_v
        out_k = (part_k * SCALE).astype(BF16)
        out_v = part_v.astype(BF16)
        if c == 1:
            fin_out[0] = out_k
            fin_out[1] = out_v
            for i in range(2):
                send(fin_out.at[i], fin_in.at[i], fin_s.at[i], fin_r.at[i], partner)
        else:
            gk_ref[:, own_lanes] = out_k
            gv_ref[:, own_lanes] = out_v

    for k in range(1, ny):
        arrived(qrecv.at[k], dq_s.at[k], dq_r.at[k], ypeer[k])
    query_rows = acc_q[y]
    for k in range(1, ny):
        query_rows += qrecv[k].astype(F32)
    out_q = jnp.transpose(query_rows * SCALE).astype(BF16)
    fin_out[2] = out_q[T:]
    send(fin_out.at[2], fin_in.at[2], fin_s.at[2], fin_r.at[2], partner)
    gq_ref[:, own_lanes] = out_q[:T]
    for i, ref in enumerate((gk_ref, gv_ref, gq_ref)):
        arrived(fin_in.at[i], fin_s.at[i], fin_r.at[i], partner)
        ref[:, other_lanes] = fin_in[i]

    for copy in started:
        copy.wait_send()


def shards(ny, nz, queries, keys, values, out_grad, w_out, frame_index, group_order):
    half = nz // 2
    width = out_grad.shape[1]
    cols = width // (2 * ny)
    zcols = cols // nz
    pairs = group_order.shape[0] // 2
    frames_in = frame_index.reshape(pairs, T)
    order_in = group_order.reshape(1, 2 * pairs)
    vmem = pltpu.VMEM
    dma = pltpu.SemaphoreType.DMA
    any_spec = pl.BlockSpec(memory_space=pl.ANY)
    out_spec = pl.BlockSpec(memory_space=pltpu.VMEM)
    plane = 2 * ny - 1
    return pl.pallas_call(
        functools.partial(kernel, ny, nz),
        out_shape=(
            jax.ShapeDtypeStruct((T, 2 * HD), BF16),
            jax.ShapeDtypeStruct((T, 2 * HD), BF16),
            jax.ShapeDtypeStruct((T, 2 * HD), BF16),
            jax.ShapeDtypeStruct((2 * HD, zcols), F32),
        ),
        in_specs=[any_spec] * 7,
        out_specs=(out_spec,) * 4,
        scratch_shapes=[
            vmem((T, 2 * HD), BF16),
            vmem((T, 2 * HD), BF16),
            vmem((T, 2 * HD), BF16),
            vmem((T, width), BF16),
            vmem((2 * HD, width), BF16),
            vmem((pairs, T), jnp.int32),
            vmem((1, 2 * pairs), jnp.int32),
            vmem((T, 2 * HD), BF16),
            vmem((nz, 2, 2, T, HD), BF16),
            vmem((ny, 2, 2, T, HD), BF16),
            vmem((pairs, T), F32),
            vmem((nz, B, T), F32),
            vmem((ny, B), F32),
            vmem((nz, ny, B, B), F32),
            vmem((nz, ny, B, B), F32),
            vmem((nz, ny, HD, B), F32),
            vmem((nz, ny, B), F32),
            vmem((nz, ny, B), F32),
            vmem((nz, ny, B), F32),
            vmem((ny, 3, ny, B), F32),
            vmem((nz, ny, B), F32),
            vmem((ny, B), F32),
            vmem((ny, HD, B), BF16),
            vmem((ny, HD, B), BF16),
            vmem((2, ny, HD, B), BF16),
            vmem((ny, 2, T, cols), BF16),
            vmem((nz, zcols, 2 * HD), F32),
            vmem((nz, zcols, 2 * HD), F32),
            vmem((B, HD), F32),
            vmem((B, HD), F32),
            vmem((ny, HD, B), F32),
            vmem((2, half, 2, T, HD), BF16),
            vmem((2, half, 2, T, HD), BF16),
            vmem((2, half, 2, T, HD), F32),
            vmem((2, half, 2, T, HD), F32),
            vmem((ny, HD, B), BF16),
            vmem((ny, HD, B), BF16),
            vmem((3, T, HD), BF16),
            vmem((3, T, HD), BF16),
            dma((7,)),
            dma((4,)),
            dma((4,)),
            dma((2, half, 2)),
            dma((nz, 2)),
            dma((ny, 2)),
            dma((ny, 2)),
            dma((plane,)),
            dma((2, ny)),
            dma((ny,)),
            dma((ny,)),
            dma((ny,)),
            dma((ny,)),
            dma((plane,)),
            dma((2, ny)),
            dma((nz,)),
            dma((nz,)),
            dma((2, 2, half, 2)),
            dma((2, 2, half, 2)),
            dma((ny,)),
            dma((ny,)),
            dma((3,)),
            dma((3,)),
        ],
        compiler_params=pltpu.CompilerParams(
            collective_id=0, has_side_effects=True, vmem_limit_bytes=50 * 1024 * 1024
        ),
    )(queries, keys, values, out_grad, w_out, frames_in, order_in)


def solution(mesh):
    ny, nz = {64: (4, 8), 16: (2, 4)}[mesh.shape["ctx"]]
    placed = (
        P("ctx", "tp"),
        P("ctx", "tp"),
        P("ctx", "tp"),
        P("ctx", None),
        P("tp", None),
        P(),
        P(),
    )
    return jax.shard_map(
        functools.partial(shards, ny, nz),
        mesh=mesh,
        in_specs=placed,
        out_specs=(P("ctx", "tp"), P("ctx", "tp"), P("ctx", "tp"), P("tp", "ctx")),
        check_vma=False,
    )
```

time: 1720 us -> 83.3 us (0.05)
  waiting for transfers between devices: 1460 us -> 0 us
  local copies, waits for them, and re-layouts: 183 us -> 8.77 us
  Pallas kernels: 0 us -> 73.5 us
  matrix products: 45.5 us -> 0 us
    reduce_scatter x2 -> x0, waiting for transfers between devices: 645 us -> none  [the longest x1 327 us: shards(): lax.psum_scatter(key_parts[0].reshape(all_rows, width_dev), 'ctx', scatte...]
    all_gather x2 -> x0, waiting for transfers between devices: 501 us -> none  [the longest x1 291 us: shards(): lax.all_gather(values, 'ctx', axis=0, tiled=True)]
    unnamed x6 -> x0, waiting for transfers between devices: 314 us -> none
    gather x4 -> x0, local copies, waits for them, and re-layouts: 97.1 us -> none  [the longest x2 50.5 us: frames_of(): group_order[stored // group_rows] * group_rows + stored % group_rows]
    pallas_call x0 -> x1, Pallas kernels: none -> 73.5 us  [shards(): pl.pallas_call(functools.partial(kernel, ny, nz), out_shape=(jax.ShapeDty...]
    dot_general x58 -> x0, matrix products: 45.5 us -> none  [the longest x16 22.3 us: head_scores(): jnp.einsum('qhd,khd->hqk', query_block, key_block, preferred_element_type...]
    dynamic_slice x40 -> x0, local copies, waits for them, and re-layouts: 26 us -> none  [shards(): lax.scan(forward_step, start_state, (key_blocks, value_blocks, key_frame_...]
    dynamic_update_slice x8 -> x0, local copies, waits for them, and re-layouts: 23.5 us -> none  [shards(): lax.scan(scan_step, zero_rows, (key_blocks, value_blocks, key_frame_blocks))]
  transfers between devices with their start and end apart: 5 -> 0, of which waited for: 5 -> 0; matrix products, arithmetic and copies ran while one was open for 7% -> 0% of each run, Pallas kernels for 0% -> 0%
where the time goes in v1:
time: 83.3 us; the launch traced here: 82.9 us
  Pallas kernels  73.5 us (88%)
  local copies, waits for them, and re-layouts  8.77 us (11%)
    pallas_call x1, Pallas kernels, shards(): pl.pallas_call(functools.partial(kernel, ny, nz), out_shape=(jax.ShapeDty...  73.5 us
    unnamed x17, local copies, waits for them, and re-layouts  8.07 us

profile of v1, /device:TPU:4, one launch (start us, length us, event | category | flops | bytes accessed | tf_op | source)
XLA Modules:
  0.0 82.9 jit_solution(918612748138028181)
XLA Ops:
  0.6 0.0 copy-start.6
  0.6 0.6 copy-done.6
  1.3 0.0 copy-start
  1.3 1.2 %copy-done = bf16[256,2048]{1,0:T(8,128)(2,1)S(1)} copy-done((bf16[256,2048]{1,0:T(8,128)(2,1)S(1)}, bf16[256,2048]{1,0:T(8,128)(2,1)}, u32[]{:S(2)}) %copy-start) | copy-done | bytes 1048600
  2.5 0.0 copy-start.1
  2.5 1.0 %copy-done.1 = bf16[128,2048]{1,0:T(8,128)(2,1)S(1)} copy-done((bf16[128,2048]{1,0:T(8,128)(2,1)S(1)}, bf16[128,2048]{1,0:T(8,128)(2,1)}, u32[]{:S(2)}) %copy-start.1) | copy-done | bytes 524312
  3.6 0.0 copy-start.2
  3.6 0.8 %copy-done.2 = bf16[128,256]{1,0:T(8,128)(2,1)S(1)} copy-done((bf16[128,256]{1,0:T(8,128)(2,1)S(1)}, bf16[128,256]{1,0:T(8,128)(2,1)}, u32[]{:S(2)}) %copy-start.2) | copy-done | bytes 65560
  4.4 0.0 copy-start.3
  4.4 0.8 %copy-done.3 = bf16[128,256]{1,0:T(8,128)(2,1)S(1)} copy-done((bf16[128,256]{1,0:T(8,128)(2,1)S(1)}, bf16[128,256]{1,0:T(8,128)(2,1)}, u32[]{:S(2)}) %copy-start.3) | copy-done | bytes 65560
  5.2 0.0 copy-start.4
  5.2 0.8 %copy-done.4 = bf16[128,256]{1,0:T(8,128)(2,1)S(1)} copy-done((bf16[128,256]{1,0:T(8,128)(2,1)S(1)}, bf16[128,256]{1,0:T(8,128)(2,1)}, u32[]{:S(2)}) %copy-start.4) | copy-done | bytes 65560
  6.1 0.0 copy-start.5
  6.1 0.8 copy-done.5
  6.8 73.5 %shard_map.102 = (bf16[128,256]{1,0:T(8,128)(2,1)S(1)}, bf16[128,256]{1,0:T(8,128)(2,1)S(1)}, bf16[128,256]{1,0:T(8,128)(2,1)S(1)}, f32[256,32]{1,0:T(8,128)S(1)}) custom-call(bf16[128,256]{1,0:T(8,128)(2,1)S(1)} %copy-done.2, bf16[128,256]{1,0:T(8,128)(2,1)S(1)} %copy-done.3, bf16[128,256]{1,0:T(8,128)(2,1)S(1)} %copy-done.4, ...), custom_call_target="tpu_custom_call" | custom-call | tf_op jit(solution)/shard_map/pallas_call | solution.py:512
  80.3 0.7 copy.11
  81.0 0.6 copy.15
  81.7 0.6 copy.16
  82.3 0.6 copy.17
Async XLA Ops:
  0.6 0.7 copy-start.6
  1.3 1.2 %copy-start = (bf16[256,2048]{1,0:T(8,128)(2,1)S(1)}, bf16[256,2048]{1,0:T(8,128)(2,1)}, u32[]{:S(2)}) copy-start(bf16[256,2048]{1,0:T(8,128)(2,1)} %w_hbm.1) | copy-start | bytes 3145732
  2.5 1.0 %copy-start.1 = (bf16[128,2048]{1,0:T(8,128)(2,1)S(1)}, bf16[128,2048]{1,0:T(8,128)(2,1)}, u32[]{:S(2)}) copy-start(bf16[128,2048]{1,0:T(8,128)(2,1)} %og_hbm.1) | copy-start | bytes 1572868
  3.6 0.8 %copy-start.2 = (bf16[128,256]{1,0:T(8,128)(2,1)S(1)}, bf16[128,256]{1,0:T(8,128)(2,1)}, u32[]{:S(2)}) copy-start(bf16[128,256]{1,0:T(8,128)(2,1)} %q_hbm.1) | copy-start | bytes 196612
  4.4 0.8 %copy-start.3 = (bf16[128,256]{1,0:T(8,128)(2,1)S(1)}, bf16[128,256]{1,0:T(8,128)(2,1)}, u32[]{:S(2)}) copy-start(bf16[128,256]{1,0:T(8,128)(2,1)} %k_hbm.1) | copy-start | bytes 196612
  5.2 0.8 %copy-start.4 = (bf16[128,256]{1,0:T(8,128)(2,1)S(1)}, bf16[128,256]{1,0:T(8,128)(2,1)}, u32[]{:S(2)}) copy-start(bf16[128,256]{1,0:T(8,128)(2,1)} %v_hbm.1) | copy-start | bytes 196612
  6.1 0.8 copy-start.5

commit v2 on v1

v2 whole, which is shorter than its diff:
```python
import functools
import math

import jax
import jax.numpy as jnp
from jax import lax
from jax.experimental import pallas as pl
from jax.experimental.pallas import tpu as pltpu
from jax.sharding import PartitionSpec as P

HD = 128
T = 128
B = 2 * T
MASKED = -1e30
FLOOR = -1e29
SCALE = HD**-0.5
EXP2_SCALE = SCALE * math.log2(math.e)
F32 = jnp.float32
BF16 = jnp.bfloat16
NT = (((1,), (1,)), ((), ()))
TN = (((0,), (0,)), ((), ()))
MESH = pl.DeviceIdType.MESH


def dot(a, b):
    return jnp.dot(a, b, preferred_element_type=F32)


def dot_general(a, b, dims):
    return lax.dot_general(a, b, dims, preferred_element_type=F32)


def kernel(
    ny,
    nz,
    q_hbm,
    k_hbm,
    v_hbm,
    og_hbm,
    w_hbm,
    fi_hbm,
    go_hbm,
    gq_ref,
    gk_ref,
    gv_ref,
    gw_ref,
    q_in,
    k_in,
    v_in,
    og_in,
    w_in,
    fi_in,
    go_in,
    da,
    kv_other,
    qd_other,
    kv,
    qd,
    frames,
    kf,
    qf,
    wts,
    dps,
    obuf,
    mst,
    lst,
    dst,
    stats,
    cst,
    ysh,
    dlt,
    osend,
    orecv,
    att,
    ogb,
    gsend,
    grecv,
    acc_k,
    acc_v,
    acc_q,
    rsk_out,
    rsk_in,
    rsv_out,
    rsv_in,
    qsend,
    qrecv,
    finv_out,
    finv_in,
    fink_out,
    fink_in,
    in_sem,
    sent,
    z_r,
    y_r,
    og_r,
    st_r,
    o_r,
    att_r,
    g_r,
    rs_r,
    dq_r,
    fin_r,
):
    half = nz // 2
    me = lax.axis_index("ctx")
    x = me // (ny * nz)
    y = lax.rem(me // nz, ny)
    z = lax.rem(me, nz)
    px = 1 - x
    cols = og_in.shape[1] // (2 * ny)
    zcols = cols // nz

    def at(xx, yy, zz):
        return xx * (ny * nz) + yy * nz + zz

    partner = at(px, y, z)
    right = at(x, y, lax.rem(z + 1, nz))
    left = at(x, y, lax.rem(z + nz - 1, nz))
    ypos = [lax.rem(y + k, ny) for k in range(ny)]
    ypeer = [at(x, ypos[k], z) for k in range(ny)]
    ydiag = [at(px, ypos[k], z) for k in range(ny)]
    zpos = [lax.rem(z + k, nz) for k in range(nz)]
    zpeer = [at(x, y, zpos[k]) for k in range(nz)]
    zdiag = [at(px, y, zpos[k]) for k in range(nz)]

    started = []

    def send(src, dst_ref, r_sem, device):
        copy = pltpu.make_async_remote_copy(
            src_ref=src,
            dst_ref=dst_ref,
            send_sem=sent.at[len(started)],
            recv_sem=r_sem,
            device_id={"ctx": device},
            device_id_type=MESH,
        )
        copy.start()
        started.append(copy)

    def arrived(dst_ref, r_sem):
        pltpu.make_async_remote_copy(
            src_ref=dst_ref,
            dst_ref=dst_ref,
            send_sem=sent.at[0],
            recv_sem=r_sem,
            device_id={"ctx": partner},
            device_id_type=MESH,
        ).wait_recv()

    loads = [
        pltpu.make_async_copy(src, to, in_sem.at[i])
        for i, (src, to) in enumerate(
            [
                (k_hbm, k_in),
                (v_hbm, v_in),
                (w_hbm, w_in),
                (og_hbm, og_in),
                (q_hbm, q_in),
                (fi_hbm, fi_in),
                (go_hbm, go_in),
            ]
        )
    ]
    for load in loads:
        load.start()
    barrier = pltpu.get_barrier_semaphore()
    peers = ydiag + ypeer[1:] + zpeer[1:] + [zdiag[k] for k in sorted({1, 2, nz - 2, nz - 1})]
    for peer in peers:
        pl.semaphore_signal(barrier, inc=1, device_id={"ctx": peer}, device_id_type=MESH)
    own_lanes = pl.ds(pl.multiple_of(x * HD, HD), HD)
    other_lanes = pl.ds(pl.multiple_of(px * HD, HD), HD)

    def stage(src, own, other, i):
        own[i] = src[:, own_lanes]
        other[i] = src[:, other_lanes]

    loads[0].wait()
    loads[1].wait()
    stage(k_in, kv.at[0, 0], kv_other, 0)
    stage(v_in, kv.at[0, 0], kv_other, 1)
    pl.semaphore_wait(barrier, len(peers))

    def left_slot(s):
        return s if s < half else nz - 1

    def right_slot(s):
        return half - 1 + s if s < half else nz - 1

    reach = min(2, half - 1)

    def kv_first(distance, way, c):
        slot = (left_slot, right_slot)[way](distance)
        k = distance if way == 0 else nz - distance
        send(kv.at[0, 0] if c == 0 else kv_other, kv.at[slot, c], z_r.at[slot, c], (zpeer, zdiag)[c][k])

    for c in range(2):
        for d in range(reach, 0, -1):
            for way in range(2):
                kv_first(d, way, c)
    send(kv_other, kv.at[0, 1], z_r.at[0, 1], partner)
    if half == 2:
        kv_first(2, 0, 0)
        kv_first(2, 1, 1)

    def z_arrived(slot, c):
        arrived(kv.at[slot, c], z_r.at[slot, c])

    def pass_on(c):
        for way in range(2):
            slot = (left_slot, right_slot)[way](2)
            z_arrived(slot, c)
            for d in (3, 4):
                if d < half or (d == half and way == c):
                    to = (left_slot, right_slot)[way](d)
                    k = d - 2 if way == 0 else nz - (d - 2)
                    send(kv.at[slot, c], kv.at[to, c], z_r.at[to, c], zpeer[k])

    for load in loads[2:]:
        load.wait()
    da[...] = dot_general(og_in[...], w_in[...], NT).astype(BF16)
    stage(q_in, qd.at[y, 0], qd_other, 0)
    stage(da, qd.at[y, 0], qd_other, 1)
    for k in range(1, ny):
        send(qd.at[y, 0], qd.at[y, 0], y_r.at[ny - k, 0], ypeer[k])
    for k in range(ny):
        send(qd_other, qd.at[y, 1], y_r.at[(ny - k) % ny, 1], ydiag[k])

    go = go_in[...]
    fi = fi_in[...].astype(F32)
    pairs, lanes = fi.shape
    groups = go.shape[1]
    half_lanes = lanes // 2
    lane = lax.broadcasted_iota(jnp.int32, (pairs, lanes), 1)
    low = jnp.where(lane < half_lanes, fi, 0.0)
    high = jnp.where(lane >= half_lanes, fi, 0.0)
    low_up = jnp.concatenate([low[:, half_lanes:], low[:, :half_lanes]], axis=1)
    high_down = jnp.concatenate([high[:, half_lanes:], high[:, :half_lanes]], axis=1)
    row = lax.broadcasted_iota(jnp.int32, (pairs, groups), 0)
    holds = [(go == 2 * row + p).astype(F32).astype(BF16) for p in range(2)]
    group_id = lax.broadcasted_iota(jnp.int32, (groups, pairs), 0)
    pair_id = lax.broadcasted_iota(jnp.int32, (groups, pairs), 1)
    picks = [(group_id == 2 * pair_id + e).astype(F32).astype(BF16) for e in range(2)]
    total = jnp.zeros((pairs, lanes), F32)
    for p in range(2):
        for e in range(2):
            part = ((low, low_up), (high_down, high))[p][e]
            total += dot_general(dot(holds[p], picks[e]).astype(BF16), part.astype(BF16), TN)
    frames[...] = total
    across = jnp.transpose(total)
    device_lane = lax.broadcasted_iota(jnp.int32, (lanes, pairs), 1)
    distance = (
        [0] + [nz - s for s in range(1, half)] + [s for s in range(1, half)] + [half]
    )
    for slot in range(nz):
        for c in range(2):
            source = at(x if c == 0 else px, y, zpos[distance[slot]])
            column = jnp.sum(jnp.where(device_lane == source, across, 0.0), axis=1, keepdims=True)
            kf[slot, pl.ds(c * T, T), :] = jnp.broadcast_to(column, (T, lanes))
    for b in range(ny):
        qf[pl.ds(b, 1), pl.ds(0, T)] = frames[pl.ds(at(x, b, z), 1), :]
        qf[pl.ds(b, 1), pl.ds(T, T)] = frames[pl.ds(at(px, b, z), 1), :]

    def og_lanes(xx, yy):
        return pl.ds(pl.multiple_of((xx * ny + yy) * cols, cols), cols)

    og_targets = [(x, k, ypeer[k]) for k in range(1, ny)] + [(px, k, ydiag[k]) for k in range(ny)]

    def og_send():
        ogb[y, x] = og_in[:, og_lanes(x, y)]
        for i, (xx, k, device) in enumerate(og_targets):
            side = 0 if i < ny - 1 else 1
            r = (ny - k) % ny
            send(
                og_in.at[:, og_lanes(xx, ypos[k])],
                ogb.at[y, x],
                og_r.at[side, r],
                device,
            )

    def forward(slot):
        kb = kv[slot, :, 0].reshape(B, HD)
        vb = kv[slot, :, 1].reshape(B, HD)
        v_t = jnp.transpose(vb)
        key_frames = jnp.concatenate([kf[slot], kf[slot]], axis=1)

        def body(b, carry):
            scores = dot_general(kb, qd[b, :, 0].reshape(B, HD), NT)
            grads = dot_general(vb, qd[b, :, 1].reshape(B, HD), NT)
            scores = jnp.where(key_frames <= qf[pl.ds(b, 1), :], scores, MASKED)
            top = jnp.maximum(jnp.max(scores, axis=0, keepdims=True), FLOOR)
            weights = jnp.exp2((scores - top) * EXP2_SCALE)
            wts[slot, b] = weights
            dps[slot, b] = grads
            mst[slot, pl.ds(b, 1), :] = top
            lst[slot, pl.ds(b, 1), :] = jnp.sum(weights, axis=0, keepdims=True)
            dst[slot, pl.ds(b, 1), :] = jnp.sum(weights * grads, axis=0, keepdims=True)
            obuf[slot, b] = dot(v_t, weights.astype(BF16))
            return carry

        lax.fori_loop(0, ny, body, 0, unroll=True)

    if half > 2:
        pass_on(0)
        pass_on(1)
    z_arrived(0, 1)
    for k in range(ny):
        for c in range(2):
            if k + c > 0:
                arrived(qd.at[ypos[k], c], y_r.at[k, c])
    og_send()
    forward(0)
    for s in range(1, half):
        for slot in (left_slot(s), right_slot(s)):
            if s != 2 or half == 2:
                z_arrived(slot, 0)
                z_arrived(slot, 1)
            forward(slot)
    z_arrived(nz - 1, 0)
    z_arrived(nz - 1, 1)
    forward(nz - 1)

    tops = mst[...]
    own_top = jnp.max(tops, axis=0)
    shares = jnp.exp2((tops - own_top[None]) * EXP2_SCALE)
    stats[y, 0] = own_top
    stats[y, 1] = jnp.sum(shares * lst[...], axis=0)
    stats[y, 2] = jnp.sum(shares * dst[...], axis=0)
    for k in range(1, ny):
        send(stats.at[y], stats.at[y], st_r.at[ny - k], ypeer[k])

    cst[...] = shares

    def attended_part(b, carry):
        part = obuf[0, b] * cst[0, pl.ds(b, 1), :]
        for slot in range(1, nz):
            part += obuf[slot, b] * cst[slot, pl.ds(b, 1), :]
        osend[b] = part.astype(BF16)
        return carry

    lax.fori_loop(0, ny, attended_part, 0)
    for k in range(1, ny):
        send(osend.at[ypos[k]], orecv.at[ny - k], o_r.at[ny - k], ypeer[k])

    for k in range(1, ny):
        arrived(stats.at[ypos[k]], st_r.at[k])
    all_top = stats[0, 0]
    for b in range(1, ny):
        all_top = jnp.maximum(all_top, stats[b, 0])
    row_total = jnp.zeros_like(all_top)
    delta = jnp.zeros_like(all_top)
    for b in range(ny):
        share = jnp.exp2((stats[b, 0] - all_top) * EXP2_SCALE)
        row_total += share * stats[b, 1]
        delta += share * stats[b, 2]
        ysh[b] = share
    inverse = 1.0 / row_total
    for b in range(ny):
        ysh[b] = ysh[b] * inverse
    dlt[...] = delta * inverse
    cst[...] = jnp.exp2((tops - all_top[None]) * EXP2_SCALE) * inverse[None]

    acc_q[...] = jnp.zeros_like(acc_q)

    def backward(slot):
        k_t = jnp.transpose(kv[slot, :, 0].reshape(B, HD))
        acc_k[slot] = jnp.zeros((B, HD), F32)
        acc_v[slot] = jnp.zeros((B, HD), F32)

        def body(b, carry):
            probs = wts[slot, b] * cst[slot, pl.ds(b, 1), :]
            grad_scores = (probs * (dps[slot, b] - dlt[pl.ds(b, 1), :])).astype(BF16)
            acc_v[slot] += dot(probs.astype(BF16), qd[b, :, 1].reshape(B, HD))
            acc_k[slot] += dot(grad_scores, qd[b, :, 0].reshape(B, HD))
            acc_q[b] += dot(k_t, grad_scores)
            return carry

        lax.fori_loop(0, ny, body, 0, unroll=True)

    def reduce_send(way, step, c, arrival):
        d = half + 1 - step
        i = step - 1
        slot = (right_slot, left_slot)[way](d)
        k = 1 if way == 0 else nz - 1
        device = zdiag[k] if step == half and c == 1 else zpeer[k]
        for t, (acc, src, to) in enumerate(((acc_v, rsv_out, rsv_in), (acc_k, rsk_out, rsk_in))):
            part = acc[slot, pl.ds(c * T, T), :]
            if arrival:
                arrived(to.at[way, i - 1, c], rs_r.at[t, way, i - 1, c])
                part += to[way, i - 1, c].astype(F32)
            src[way, i, c] = part.astype(src.dtype)
            send(src.at[way, i, c], to.at[way, i, c], rs_r.at[t, way, i, c], device)

    def reduce_rest(step):
        if step > 2:
            reduce_send(0, step, 1, True)
            reduce_send(1, step, 0, True)
        reduce_send(0, step, 0, True)
        reduce_send(1, step, 1, True)

    def attended_rows():
        for k in range(1, ny):
            arrived(orecv.at[k], o_r.at[k])
        rows_att = osend[y].astype(F32) * ysh[y, pl.ds(y, 1), :]
        for k in range(1, ny):
            rows_att += orecv[k].astype(F32) * ysh[ypos[k], pl.ds(y, 1), :]
        att[x, y] = rows_att.astype(BF16)
        for i, (xx, k, device) in enumerate(og_targets):
            side = 0 if i < ny - 1 else 1
            send(att.at[x, y], att.at[x, y], att_r.at[side, (ny - k) % ny], device)

    def query_part():
        backward(0)
        for t, (acc, src, to) in enumerate(((acc_v, finv_out, finv_in), (acc_k, fink_out, fink_in))):
            src[...] = acc[0, pl.ds(T, T), :].astype(src.dtype)
            send(src, to, fin_r.at[t], partner)
        for b in range(ny):
            for c in range(2):
                qsend[b, c] = acc_q[b, :, pl.ds(c * T, T)].astype(BF16)
        for k in range(ny):
            r = (ny - k) % ny
            if k > 0:
                send(qsend.at[ypos[k], 0], qrecv.at[0, r], dq_r.at[0, r], ypeer[k])
            send(qsend.at[ypos[k], 1], qrecv.at[1, r], dq_r.at[1, r], ydiag[k])

    def weight_part():
        for i, (xx, k, device) in enumerate(og_targets):
            side = 0 if i < ny - 1 else 1
            source_x = x if side == 0 else px
            arrived(ogb.at[ypos[k], source_x], og_r.at[side, k])
            arrived(att.at[source_x, ypos[k]], att_r.at[side, k])
        for h in range(2):
            part = jnp.zeros((HD, cols), F32)
            for b in range(ny):
                for c in range(2):
                    part += dot(att[h, b, :, pl.ds(c * T, T)], ogb[b, h ^ c])
            gsend[:, :, pl.ds(h * HD, HD)] = jnp.transpose(part).reshape(nz, zcols, HD)
        for k in range(1, nz):
            send(gsend.at[zpos[k]], grecv.at[nz - k], g_r.at[nz - k], zpeer[k])

    backward(nz - 1)
    reduce_send(0, 1, 0, False)
    reduce_send(1, 1, 1, False)
    backward(right_slot(half - 1))
    reduce_send(0, 2, 1, False)
    backward(left_slot(half - 1))
    reduce_send(1, 2, 0, False)
    if half > 2:
        backward(right_slot(half - 2))
    attended_rows()
    if half > 2:
        backward(left_slot(half - 2))
    reduce_rest(2)
    for step in range(3, half + 1):
        if step < half:
            backward(right_slot(half - step))
            backward(left_slot(half - step))
        if step == half:
            query_part()
        reduce_rest(step)
        if step == 3:
            weight_part()
    if half == 2:
        query_part()
        weight_part()

    for t, (acc, src, to) in enumerate(((acc_v, finv_out, finv_in), (acc_k, fink_out, fink_in))):
        arrived(to, fin_r.at[t])
    for k in range(ny):
        for c in range(2):
            if k + c > 0:
                arrived(qrecv.at[c, k], dq_r.at[c, k])
    for c, lanes_out in enumerate((own_lanes, other_lanes)):
        rows_q = qsend[y, 0].astype(F32) if c == 0 else qrecv[1, 0].astype(F32)
        for k in range(1, ny):
            rows_q += qrecv[c, k].astype(F32)
        gq_ref[:, lanes_out] = jnp.transpose(rows_q * SCALE).astype(BF16)
    for k in range(1, nz):
        arrived(grecv.at[k], g_r.at[k])
    weight_rows = gsend[z]
    for k in range(1, nz):
        weight_rows += grecv[k]
    gw_ref[...] = weight_rows
    for c, lanes_out in ((1, other_lanes), (0, own_lanes)):
        part_v = finv_in[...] if c == 1 else acc_v[0, pl.ds(0, T), :]
        part_k = fink_in[...].astype(F32) if c == 1 else acc_k[0, pl.ds(0, T), :]
        for way in (0, 1) if c == 1 else (1, 0):
            arrived(rsv_in.at[way, half - 1, c], rs_r.at[0, way, half - 1, c])
            part_v += rsv_in[way, half - 1, c]
            arrived(rsk_in.at[way, half - 1, c], rs_r.at[1, way, half - 1, c])
            part_k += rsk_in[way, half - 1, c].astype(F32)
        gv_ref[:, lanes_out] = part_v.astype(BF16)
        gk_ref[:, lanes_out] = (part_k * SCALE).astype(BF16)

    for copy in started:
        copy.wait_send()


def shards(ny, nz, queries, keys, values, out_grad, w_out, frame_index, group_order):
    half = nz // 2
    width = out_grad.shape[1]
    cols = width // (2 * ny)
    zcols = cols // nz
    pairs = group_order.shape[0] // 2
    frames_in = frame_index.reshape(pairs, T)
    order_in = group_order.reshape(1, 2 * pairs)
    vmem = pltpu.VMEM
    dma = pltpu.SemaphoreType.DMA
    any_spec = pl.BlockSpec(memory_space=pltpu.HBM)
    out_spec = pl.BlockSpec(memory_space=pltpu.VMEM)
    results = pl.pallas_call(
        functools.partial(kernel, ny, nz),
        out_shape=(
            jax.ShapeDtypeStruct((T, 2 * HD), BF16),
            jax.ShapeDtypeStruct((T, 2 * HD), BF16),
            jax.ShapeDtypeStruct((T, 2 * HD), BF16),
            jax.ShapeDtypeStruct((zcols, 2 * HD), F32),
        ),
        in_specs=[any_spec] * 7,
        out_specs=(out_spec,) * 4,
        scratch_shapes=[
            vmem((T, 2 * HD), BF16),
            vmem((T, 2 * HD), BF16),
            vmem((T, 2 * HD), BF16),
            vmem((T, width), BF16),
            vmem((2 * HD, width), BF16),
            vmem((pairs, T), jnp.int32),
            vmem((1, 2 * pairs), jnp.int32),
            vmem((T, 2 * HD), BF16),
            vmem((2, T, HD), BF16),
            vmem((2, T, HD), BF16),
            vmem((nz, 2, 2, T, HD), BF16),
            vmem((ny, 2, 2, T, HD), BF16),
            vmem((pairs, T), F32),
            vmem((nz, B, T), F32),
            vmem((ny, B), F32),
            vmem((nz, ny, B, B), F32),
            vmem((nz, ny, B, B), F32),
            vmem((nz, ny, HD, B), F32),
            vmem((nz, ny, B), F32),
            vmem((nz, ny, B), F32),
            vmem((nz, ny, B), F32),
            vmem((ny, 3, ny, B), F32),
            vmem((nz, ny, B), F32),
            vmem((ny, ny, B), F32),
            vmem((ny, B), F32),
            vmem((ny, HD, B), BF16),
            vmem((ny, HD, B), BF16),
            vmem((2, ny, HD, B), BF16),
            vmem((ny, 2, T, cols), BF16),
            vmem((nz, zcols, 2 * HD), F32),
            vmem((nz, zcols, 2 * HD), F32),
            vmem((nz, B, HD), F32),
            vmem((nz, B, HD), F32),
            vmem((ny, HD, B), F32),
            vmem((2, half, 2, T, HD), BF16),
            vmem((2, half, 2, T, HD), BF16),
            vmem((2, half, 2, T, HD), F32),
            vmem((2, half, 2, T, HD), F32),
            vmem((ny, 2, HD, T), BF16),
            vmem((2, ny, HD, T), BF16),
            vmem((T, HD), F32),
            vmem((T, HD), F32),
            vmem((T, HD), BF16),
            vmem((T, HD), BF16),
            dma((7,)),
            dma((128,)),
            dma((nz, 2)),
            dma((ny, 2)),
            dma((2, ny)),
            dma((ny,)),
            dma((ny,)),
            dma((2, ny)),
            dma((nz,)),
            dma((2, 2, half, 2)),
            dma((2, ny)),
            dma((2,)),
        ],
        compiler_params=pltpu.CompilerParams(
            collective_id=0, has_side_effects=True, vmem_limit_bytes=63 * 1024 * 1024
        ),
    )(queries, keys, values, out_grad, w_out, frames_in, order_in)
    return results[:3] + (jnp.transpose(results[3]),)


def solution(mesh):
    ny, nz = {64: (4, 8), 32: (2, 8), 16: (2, 4)}[mesh.shape["ctx"]]
    placed = (
        P("ctx", "tp"),
        P("ctx", "tp"),
        P("ctx", "tp"),
        P("ctx", None),
        P("tp", None),
        P(),
        P(),
    )
    return jax.shard_map(
        functools.partial(shards, ny, nz),
        mesh=mesh,
        in_specs=placed,
        out_specs=(P("ctx", "tp"), P("ctx", "tp"), P("ctx", "tp"), P("tp", "ctx")),
        check_vma=False,
    )
```

time: 83.3 us -> 65 us (0.78)
  Pallas kernels: 73.5 us -> 60.3 us
  local copies, waits for them, and re-layouts: 8.77 us -> 3.74 us
    pallas_call x1, Pallas kernels: 73.5 us -> 60.3 us  [shards(): pl.pallas_call(functools.partial(kernel, ny, nz), out_shape=(jax.ShapeDty...]
    unnamed x17 -> x10, local copies, waits for them, and re-layouts: 8.07 us -> 3.74 us
where the time goes in v2:
time: 65 us; the launch traced here: 64.7 us
  Pallas kernels  60.3 us (93%)
  local copies, waits for them, and re-layouts  3.74 us (6%)
  between operations  0.65 us (1%)
    pallas_call x1, Pallas kernels, shards(): pl.pallas_call(functools.partial(kernel, ny, nz), out_shape=(jax.ShapeDty...  60.3 us
    unnamed x10, local copies, waits for them, and re-layouts  3.74 us

profile of v2, /device:TPU:4, one launch (start us, length us, event | category | flops | bytes accessed | tf_op | source)
XLA Modules:
  0.0 64.7 jit_solution(15518448925297804101)
XLA Ops:
  0.6 60.3 %shard_map.102 = (bf16[128,256]{1,0:T(8,128)(2,1)}, bf16[128,256]{1,0:T(8,128)(2,1)}, bf16[128,256]{1,0:T(8,128)(2,1)}, f32[32,256]{1,0:T(8,128)}) custom-call(bf16[128,256]{1,0:T(8,128)(2,1)} %q_hbm.1, bf16[128,256]{1,0:T(8,128)(2,1)} %k_hbm.1, bf16[128,256]{1,0:T(8,128)(2,1)} %v_hbm.1, bf16[128,2048]{1,0:T(8,128)(2,1)} %og_hbm.1, bf16[256,2048]{1,0:T(8,128)(2,1)} %w_hbm.1, ...), custom_call_target="tpu_custom_call" | custom-call | tf_op jit(solution)/shard_map/pallas_call | solution.py:510
  61.0 0.0 copy-start.1
  61.0 1.5 %copy.15 = bf16[128,256]{1,0:T(8,128)(2,1)} copy(bf16[128,256]{1,0:T(8,128)(2,1)} %get-tuple-element.16) | data formatting | bytes 131072
  62.5 0.0 copy-done.1
  62.5 0.0 copy-start
  62.5 0.6 copy.16
  63.1 0.2 copy-done
  63.3 0.0 copy-start.2
  63.3 0.6 copy.17
  64.0 0.1 copy-done.2
  64.1 0.6 copy.18
Async XLA Ops:
  61.0 1.5 %copy-start.1 = (bf16[128,256]{1,0:T(8,128)(2,1)S(1)}, bf16[128,256]{1,0:T(8,128)(2,1)}, u32[]{:S(2)}) copy-start(bf16[128,256]{1,0:T(8,128)(2,1)} %get-tuple-element.17) | copy-start | bytes 196612
  62.5 0.9 %copy-start = (bf16[128,256]{1,0:T(8,128)(2,1)S(1)}, bf16[128,256]{1,0:T(8,128)(2,1)}, u32[]{:S(2)}) copy-start(bf16[128,256]{1,0:T(8,128)(2,1)} %get-tuple-element.18) | copy-start | bytes 196612
  63.3 0.8 %copy-start.2 = (f32[32,256]{1,0:T(8,128)S(1)}, f32[32,256]{1,0:T(8,128)}, u32[]{:S(2)}) copy-start(f32[32,256]{1,0:T(8,128)} %get-tuple-element.11) | copy-start | bytes 98308

commit v3 on v2

--- a/solution.py
+++ b/solution.py
@@ -40,9 +40,7 @@
     w_hbm,
     fi_hbm,
     go_hbm,
-    gq_ref,
-    gk_ref,
-    gv_ref,
+    out_ref,
     gw_ref,
     q_in,
     k_in,
@@ -61,7 +59,7 @@
     qf,
     wts,
     dps,
-    obuf,
+    v_t,
     mst,
     lst,
     dst,
@@ -101,6 +99,7 @@
     dq_r,
     fin_r,
 ):
+    gq_ref, gk_ref, gv_ref = (out_ref.at[:, pl.ds(i * B, B)] for i in range(3))
     half = nz // 2
     me = lax.axis_index("ctx")
     x = me // (ny * nz)
@@ -164,7 +163,7 @@
     for load in loads:
         load.start()
     barrier = pltpu.get_barrier_semaphore()
-    peers = ydiag + ypeer[1:] + zpeer[1:] + [zdiag[k] for k in sorted({1, 2, nz - 2, nz - 1})]
+    peers = ydiag + ypeer[1:] + zpeer[1:] + [zdiag[1], zdiag[nz - 1]]
     for peer in peers:
         pl.semaphore_signal(barrier, inc=1, device_id={"ctx": peer}, device_id_type=MESH)
     own_lanes = pl.ds(pl.multiple_of(x * HD, HD), HD)
@@ -174,56 +173,13 @@
         own[i] = src[:, own_lanes]
         other[i] = src[:, other_lanes]
 
-    loads[0].wait()
-    loads[1].wait()
+    for load in loads:
+        load.wait()
     stage(k_in, kv.at[0, 0], kv_other, 0)
     stage(v_in, kv.at[0, 0], kv_other, 1)
-    pl.semaphore_wait(barrier, len(peers))
-
-    def left_slot(s):
-        return s if s < half else nz - 1
-
-    def right_slot(s):
-        return half - 1 + s if s < half else nz - 1
-
-    reach = min(2, half - 1)
-
-    def kv_first(distance, way, c):
-        slot = (left_slot, right_slot)[way](distance)
-        k = distance if way == 0 else nz - distance
-        send(kv.at[0, 0] if c == 0 else kv_other, kv.at[slot, c], z_r.at[slot, c], (zpeer, zdiag)[c][k])
-
-    for c in range(2):
-        for d in range(reach, 0, -1):
-            for way in range(2):
-                kv_first(d, way, c)
-    send(kv_other, kv.at[0, 1], z_r.at[0, 1], partner)
-    if half == 2:
-        kv_first(2, 0, 0)
-        kv_first(2, 1, 1)
-
-    def z_arrived(slot, c):
-        arrived(kv.at[slot, c], z_r.at[slot, c])
-
-    def pass_on(c):
-        for way in range(2):
-            slot = (left_slot, right_slot)[way](2)
-            z_arrived(slot, c)
-            for d in (3, 4):
-                if d < half or (d == half and way == c):
-                    to = (left_slot, right_slot)[way](d)
-                    k = d - 2 if way == 0 else nz - (d - 2)
-                    send(kv.at[slot, c], kv.at[to, c], z_r.at[to, c], zpeer[k])
-
-    for load in loads[2:]:
-        load.wait()
     da[...] = dot_general(og_in[...], w_in[...], NT).astype(BF16)
     stage(q_in, qd.at[y, 0], qd_other, 0)
     stage(da, qd.at[y, 0], qd_other, 1)
-    for k in range(1, ny):
-        send(qd.at[y, 0], qd.at[y, 0], y_r.at[ny - k, 0], ypeer[k])
-    for k in range(ny):
-        send(qd_other, qd.at[y, 1], y_r.at[(ny - k) % ny, 1], ydiag[k])
 
     go = go_in[...]
     fi = fi_in[...].astype(F32)
@@ -260,6 +216,44 @@
         qf[pl.ds(b, 1), pl.ds(0, T)] = frames[pl.ds(at(x, b, z), 1), :]
         qf[pl.ds(b, 1), pl.ds(T, T)] = frames[pl.ds(at(px, b, z), 1), :]
 
+    pl.semaphore_wait(barrier, len(peers))
+
+    def left_slot(s):
+        return s if s < half else nz - 1
+
+    def right_slot(s):
+        return half - 1 + s if s < half else nz - 1
+
+    def z_send(way, s, c):
+        slots = (left_slot, right_slot)[way]
+        k = 1 if way == 0 else nz - 1
+        slot = slots(s)
+        if s > 1:
+            send(kv.at[slots(s - 1), c], kv.at[slot, c], z_r.at[slot, c], zpeer[k])
+        elif c == 0:
+            send(kv.at[0, 0], kv.at[slot, 0], z_r.at[slot, 0], zpeer[k])
+        else:
+            send(kv_other, kv.at[slot, 1], z_r.at[slot, 1], zdiag[k])
+
+    def z_arrived(slot, c):
+        arrived(kv.at[slot, c], z_r.at[slot, c])
+
+    def relay(s):
+        for c in range(2):
+            for way in range(2):
+                z_arrived((left_slot, right_slot)[way](s), c)
+                if s + 1 < half or way == c:
+                    z_send(way, s + 1, c)
+
+    for c in range(2):
+        for way in range(2):
+            z_send(way, 1, c)
+    for k in range(1, ny):
+        send(qd.at[y, 0], qd.at[y, 0], y_r.at[ny - k, 0], ypeer[k])
+    for k in range(ny):
+        send(qd_other, qd.at[y, 1], y_r.at[(ny - k) % ny, 1], ydiag[k])
+    send(kv_other, kv.at[0, 1], z_r.at[0, 1], partner)
+
     def og_lanes(xx, yy):
         return pl.ds(pl.multiple_of((xx * ny + yy) * cols, cols), cols)
 
@@ -280,7 +274,7 @@
     def forward(slot):
         kb = kv[slot, :, 0].reshape(B, HD)
         vb = kv[slot, :, 1].reshape(B, HD)
-        v_t = jnp.transpose(vb)
+        v_t[slot] = jnp.transpose(vb)
         key_frames = jnp.concatenate([kf[slot], kf[slot]], axis=1)
 
         def body(b, carry):
@@ -294,14 +288,12 @@
             mst[slot, pl.ds(b, 1), :] = top
             lst[slot, pl.ds(b, 1), :] = jnp.sum(weights, axis=0, keepdims=True)
             dst[slot, pl.ds(b, 1), :] = jnp.sum(weights * grads, axis=0, keepdims=True)
-            obuf[slot, b] = dot(v_t, weights.astype(BF16))
             return carry
 
         lax.fori_loop(0, ny, body, 0, unroll=True)
 
-    if half > 2:
-        pass_on(0)
-        pass_on(1)
+    for s in range(1, max(half - 1, 2)):
+        relay(s)
     z_arrived(0, 1)
     for k in range(ny):
         for c in range(2):
@@ -310,11 +302,10 @@
     og_send()
     forward(0)
     for s in range(1, half):
-        for slot in (left_slot(s), right_slot(s)):
-            if s != 2 or half == 2:
-                z_arrived(slot, 0)
-                z_arrived(slot, 1)
-            forward(slot)
+        if s > 1 and s == half - 1:
+            relay(s)
+        forward(left_slot(s))
+        forward(right_slot(s))
     z_arrived(nz - 1, 0)
     z_arrived(nz - 1, 1)
     forward(nz - 1)
@@ -330,16 +321,14 @@
 
     cst[...] = shares
 
-    def attended_part(b, carry):
-        part = obuf[0, b] * cst[0, pl.ds(b, 1), :]
-        for slot in range(1, nz):
-            part += obuf[slot, b] * cst[slot, pl.ds(b, 1), :]
+    for k in [*range(1, ny), 0]:
+        b = ypos[k]
+        part = jnp.zeros((HD, B), F32)
+        for slot in range(nz):
+            part += dot(v_t[slot], (wts[slot, b] * cst[slot, pl.ds(b, 1), :]).astype(BF16))
         osend[b] = part.astype(BF16)
-        return carry
-
-    lax.fori_loop(0, ny, attended_part, 0)
-    for k in range(1, ny):
-        send(osend.at[ypos[k]], orecv.at[ny - k], o_r.at[ny - k], ypeer[k])
+        if k > 0:
+            send(osend.at[b], orecv.at[ny - k], o_r.at[ny - k], ypeer[k])
 
     for k in range(1, ny):
         arrived(stats.at[ypos[k]], st_r.at[k])
@@ -376,26 +365,37 @@
 
         lax.fori_loop(0, ny, body, 0, unroll=True)
 
-    def reduce_send(way, step, c, arrival):
+    pieces = (
+        (0, T // 2, acc_v, rsv_out, rsv_in),
+        (T // 2, T // 2, acc_v, rsv_out, rsv_in),
+        (0, T, acc_k, rsk_out, rsk_in),
+    )
+
+    def reduce_send(way, step, c, t, arrival):
         d = half + 1 - step
         i = step - 1
         slot = (right_slot, left_slot)[way](d)
         k = 1 if way == 0 else nz - 1
         device = zdiag[k] if step == half and c == 1 else zpeer[k]
-        for t, (acc, src, to) in enumerate(((acc_v, rsv_out, rsv_in), (acc_k, rsk_out, rsk_in))):
-            part = acc[slot, pl.ds(c * T, T), :]
-            if arrival:
-                arrived(to.at[way, i - 1, c], rs_r.at[t, way, i - 1, c])
-                part += to[way, i - 1, c].astype(F32)
-            src[way, i, c] = part.astype(src.dtype)
-            send(src.at[way, i, c], to.at[way, i, c], rs_r.at[t, way, i, c], device)
+        first, count, acc, src, to = pieces[t]
+        rows = pl.ds(first, count)
+        part = acc[slot, pl.ds(c * T + first, count), :]
+        if arrival:
+            arrived(to.at[way, i - 1, c, rows], rs_r.at[t, way, i - 1, c])
+            part += to[way, i - 1, c, rows].astype(F32)
+        src[way, i, c, rows] = part.astype(src.dtype)
+        send(src.at[way, i, c, rows], to.at[way, i, c, rows], rs_r.at[t, way, i, c], device)
+
+    def reduce_chunk(way, step, c):
+        for t in range(3):
+            reduce_send(way, step, c, t, False)
 
     def reduce_rest(step):
-        if step > 2:
-            reduce_send(0, step, 1, True)
-            reduce_send(1, step, 0, True)
-        reduce_send(0, step, 0, True)
-        reduce_send(1, step, 1, True)
+        for turn in range(2 if step > 2 else 1):
+            for t in range(3):
+                for way in range(2):
+                    last = turn == 1 or step == 2
+                    reduce_send(way, step, way if last else 1 - way, t, True)
 
     def attended_rows():
         for k in range(1, ny):
@@ -438,29 +438,22 @@
             send(gsend.at[zpos[k]], grecv.at[nz - k], g_r.at[nz - k], zpeer[k])
 
     backward(nz - 1)
-    reduce_send(0, 1, 0, False)
-    reduce_send(1, 1, 1, False)
+    reduce_chunk(0, 1, 0)
+    reduce_chunk(1, 1, 1)
     backward(right_slot(half - 1))
-    reduce_send(0, 2, 1, False)
+    reduce_chunk(0, 2, 1)
     backward(left_slot(half - 1))
-    reduce_send(1, 2, 0, False)
-    if half > 2:
-        backward(right_slot(half - 2))
+    reduce_chunk(1, 2, 0)
     attended_rows()
-    if half > 2:
-        backward(left_slot(half - 2))
-    reduce_rest(2)
-    for step in range(3, half + 1):
-        if step < half:
-            backward(right_slot(half - step))
-            backward(left_slot(half - step))
-        if step == half:
-            query_part()
+    for d in range(half - 2, 0, -1):
+        backward(right_slot(d))
+        backward(left_slot(d))
+    query_part()
+    for step in range(2, half + 1):
+        if step == max(half, 3):
+            weight_part()
         reduce_rest(step)
-        if step == 3:
-            weight_part()
     if half == 2:
-        query_part()
         weight_part()
 
     for t, (acc, src, to) in enumerate(((acc_v, finv_out, finv_in), (acc_k, fink_out, fink_in))):
@@ -474,22 +467,23 @@
         for k in range(1, ny):
             rows_q += qrecv[c, k].astype(F32)
         gq_ref[:, lanes_out] = jnp.transpose(rows_q * SCALE).astype(BF16)
+    for c, lanes_out in ((1, other_lanes), (0, own_lanes)):
+        part_v = finv_in[...] if c == 1 else acc_v[0, pl.ds(0, T), :]
+        part_k = fink_in[...].astype(F32) if c == 1 else acc_k[0, pl.ds(0, T), :]
+        for way in (0, 1) if c == 1 else (1, 0):
+            for t, (first, count, acc, src, to) in enumerate(pieces):
+                arrived(to.at[way, half - 1, c, pl.ds(first, count)], rs_r.at[t, way, half - 1, c])
+            part_v += rsv_in[way, half - 1, c]
+            part_k += rsk_in[way, half - 1, c].astype(F32)
+        gv_ref[:, lanes_out] = part_v.astype(BF16)
+        gk_ref[:, lanes_out] = (part_k * SCALE).astype(BF16)
+
     for k in range(1, nz):
         arrived(grecv.at[k], g_r.at[k])
     weight_rows = gsend[z]
     for k in range(1, nz):
         weight_rows += grecv[k]
     gw_ref[...] = weight_rows
-    for c, lanes_out in ((1, other_lanes), (0, own_lanes)):
-        part_v = finv_in[...] if c == 1 else acc_v[0, pl.ds(0, T), :]
-        part_k = fink_in[...].astype(F32) if c == 1 else acc_k[0, pl.ds(0, T), :]
-        for way in (0, 1) if c == 1 else (1, 0):
-            arrived(rsv_in.at[way, half - 1, c], rs_r.at[0, way, half - 1, c])
-            part_v += rsv_in[way, half - 1, c]
-            arrived(rsk_in.at[way, half - 1, c], rs_r.at[1, way, half - 1, c])
-            part_k += rsk_in[way, half - 1, c].astype(F32)
-        gv_ref[:, lanes_out] = part_v.astype(BF16)
-        gk_ref[:, lanes_out] = (part_k * SCALE).astype(BF16)
 
     for copy in started:
         copy.wait_send()
@@ -510,13 +504,11 @@
     results = pl.pallas_call(
         functools.partial(kernel, ny, nz),
         out_shape=(
-            jax.ShapeDtypeStruct((T, 2 * HD), BF16),
-            jax.ShapeDtypeStruct((T, 2 * HD), BF16),
-            jax.ShapeDtypeStruct((T, 2 * HD), BF16),
+            jax.ShapeDtypeStruct((T, 6 * HD), BF16),
             jax.ShapeDtypeStruct((zcols, 2 * HD), F32),
         ),
         in_specs=[any_spec] * 7,
-        out_specs=(out_spec,) * 4,
+        out_specs=(out_spec,) * 2,
         scratch_shapes=[
             vmem((T, 2 * HD), BF16),
             vmem((T, 2 * HD), BF16),
@@ -535,7 +527,7 @@
             vmem((ny, B), F32),
             vmem((nz, ny, B, B), F32),
             vmem((nz, ny, B, B), F32),
-            vmem((nz, ny, HD, B), F32),
+            vmem((nz, HD, B), BF16),
             vmem((nz, ny, B), F32),
             vmem((nz, ny, B), F32),
             vmem((nz, ny, B), F32),
@@ -563,7 +555,7 @@
             vmem((T, HD), BF16),
             vmem((T, HD), BF16),
             dma((7,)),
-            dma((128,)),
+            dma((160,)),
             dma((nz, 2)),
             dma((ny, 2)),
             dma((2, ny)),
@@ -571,7 +563,7 @@
             dma((ny,)),
             dma((2, ny)),
             dma((nz,)),
-            dma((2, 2, half, 2)),
+            dma((3, 2, half, 2)),
             dma((2, ny)),
             dma((2,)),
         ],
@@ -579,7 +571,8 @@
             collective_id=0, has_side_effects=True, vmem_limit_bytes=63 * 1024 * 1024
         ),
     )(queries, keys, values, out_grad, w_out, frames_in, order_in)
-    return results[:3] + (jnp.transpose(results[3]),)
+    o, g = results
+    return o[:, :B], o[:, B:2*B], o[:, 2*B:], jnp.transpose(g)
 
 
 def solution(mesh):

time: 65 us -> 59 us (0.908)
  Pallas kernels: 60.3 us -> 55.9 us
  local copies, waits for them, and re-layouts: 3.74 us -> 2.2 us
    pallas_call x1, Pallas kernels: 60.3 us -> 55.9 us  [shards(): pl.pallas_call(functools.partial(kernel, ny, nz), out_shape=(jax.ShapeDty...]
    unnamed x10 -> x3, local copies, waits for them, and re-layouts: 3.74 us -> 0.62 us
    slice x0 -> x1, local copies, waits for them, and re-layouts: none -> 1.59 us  [shards(): return (o[:, :B], o[:, B:2 * B], o[:, 2 * B:], jnp.transpose(g))]
where the time goes in v3:
time: 59 us; the launch traced here: 58.8 us
  Pallas kernels  55.9 us (95%)
  local copies, waits for them, and re-layouts  2.2 us (4%)
  between operations  0.65 us (1%)
    pallas_call x1, Pallas kernels, shards(): pl.pallas_call(functools.partial(kernel, ny, nz), out_shape=(jax.ShapeDty...  55.9 us
    slice x1, local copies, waits for them, and re-layouts, shards(): return (o[:, :B], o[:, B:2 * B], o[:, 2 * B:], jnp.transpose(g))  1.59 us

profile of v3, /device:TPU:4, one launch (start us, length us, event | category | flops | bytes accessed | tf_op | source)
XLA Modules:
  0.0 58.8 jit_solution(11420537336489687874)
XLA Ops:
  0.6 55.9 %shard_map.102 = (bf16[128,768]{1,0:T(8,128)(2,1)}, f32[32,256]{1,0:T(8,128)}) custom-call(bf16[128,256]{1,0:T(8,128)(2,1)} %q_hbm.1, bf16[128,256]{1,0:T(8,128)(2,1)} %k_hbm.1, bf16[128,256]{1,0:T(8,128)(2,1)} %v_hbm.1, bf16[128,2048]{1,0:T(8,128)(2,1)} %og_hbm.1, bf16[256,2048]{1,0:T(8,128)(2,1)} %w_hbm.1, s32[64,128]{1,0:T(8,128)} %bitcast.3, ...), custom_call_target="tpu_custom_call" | custom-call | tf_op jit(solution)/shard_map/pallas_call | solution.py:504
  56.6 0.0 copy-start
  56.6 1.6 %fusion = (bf16[128,256]{1,0:T(8,128)(2,1)}, bf16[128,256]{1,0:T(8,128)(2,1)}, bf16[128,256]{1,0:T(8,128)(2,1)}) fusion(bf16[128,768]{1,0:T(8,128)(2,1)} %get-tuple-element.6), kind=kLoop, calls=%fused_computation | loop fusion | bytes 393216 | tf_op jit(solution)/shard_map/slice | solution.py:575
  58.2 0.0 copy-done
  58.2 0.6 %copy.12 = f32[256,32]{0,1:T(8,128)} copy(f32[256,32]{0,1:T(8,128)S(1)} %bitcast.4) | data formatting | bytes 65536
Async XLA Ops:
  56.6 1.6 %copy-start = (f32[32,256]{1,0:T(8,128)S(1)}, f32[32,256]{1,0:T(8,128)}, u32[]{:S(2)}) copy-start(f32[32,256]{1,0:T(8,128)} %get-tuple-element.7) | copy-start | bytes 98308

commit v4 on v3

--- a/solution.py
+++ b/solution.py
@@ -238,16 +238,26 @@
     def z_arrived(slot, c):
         arrived(kv.at[slot, c], z_r.at[slot, c])
 
+    def z_send_far(way, source, peers_far):
+        k = 2 if way == 0 else nz - 2
+        send(source, kv.at[nz - 1, way], z_r.at[nz - 1, way], peers_far[k])
+
     def relay(s):
         for c in range(2):
             for way in range(2):
-                z_arrived((left_slot, right_slot)[way](s), c)
-                if s + 1 < half or way == c:
+                slot = (left_slot, right_slot)[way](s)
+                z_arrived(slot, c)
+                if s + 1 < half:
                     z_send(way, s + 1, c)
+                if s == half - 2 and way == c:
+                    z_send_far(way, kv.at[slot, c], zpeer)
 
     for c in range(2):
         for way in range(2):
             z_send(way, 1, c)
+    if half == 2:
+        z_send_far(0, kv.at[0, 0], zpeer)
+        z_send_far(1, kv_other, zdiag)
     for k in range(1, ny):
         send(qd.at[y, 0], qd.at[y, 0], y_r.at[ny - k, 0], ypeer[k])
     for k in range(ny):
@@ -366,8 +376,7 @@
         lax.fori_loop(0, ny, body, 0, unroll=True)
 
     pieces = (
-        (0, T // 2, acc_v, rsv_out, rsv_in),
-        (T // 2, T // 2, acc_v, rsv_out, rsv_in),
+        (0, T, acc_v, rsv_out, rsv_in),
         (0, T, acc_k, rsk_out, rsk_in),
     )
 
@@ -387,12 +396,12 @@
         send(src.at[way, i, c, rows], to.at[way, i, c, rows], rs_r.at[t, way, i, c], device)
 
     def reduce_chunk(way, step, c):
-        for t in range(3):
+        for t in range(2):
             reduce_send(way, step, c, t, False)
 
     def reduce_rest(step):
         for turn in range(2 if step > 2 else 1):
-            for t in range(3):
+            for t in range(2):
                 for way in range(2):
                     last = turn == 1 or step == 2
                     reduce_send(way, step, way if last else 1 - way, t, True)

time: 59 us -> 57.9 us (0.981)
  Pallas kernels: 55.9 us -> 54.9 us
    pallas_call x1, Pallas kernels: 55.9 us -> 54.9 us  [shards(): pl.pallas_call(functools.partial(kernel, ny, nz), out_shape=(jax.ShapeDty...]
where the time goes in v4:
time: 57.9 us; the launch traced here: 57.7 us
  Pallas kernels  54.9 us (95%)
  local copies, waits for them, and re-layouts  2.2 us (4%)
  between operations  0.65 us (1%)
    pallas_call x1, Pallas kernels, shards(): pl.pallas_call(functools.partial(kernel, ny, nz), out_shape=(jax.ShapeDty...  54.9 us
    slice x1, local copies, waits for them, and re-layouts, shards(): return (o[:, :B], o[:, B:2 * B], o[:, 2 * B:], jnp.transpose(g))  1.59 us

profile of v4, /device:TPU:4, one launch (start us, length us, event | category | flops | bytes accessed | tf_op | source)
XLA Modules:
  0.0 57.7 jit_solution(10384677721816160505)
XLA Ops:
  0.6 54.9 %shard_map.102 = (bf16[128,768]{1,0:T(8,128)(2,1)}, f32[32,256]{1,0:T(8,128)}) custom-call(bf16[128,256]{1,0:T(8,128)(2,1)} %q_hbm.1, bf16[128,256]{1,0:T(8,128)(2,1)} %k_hbm.1, bf16[128,256]{1,0:T(8,128)(2,1)} %v_hbm.1, bf16[128,2048]{1,0:T(8,128)(2,1)} %og_hbm.1, bf16[256,2048]{1,0:T(8,128)(2,1)} %w_hbm.1, s32[64,128]{1,0:T(8,128)} %bitcast.3, ...), custom_call_target="tpu_custom_call" | custom-call | tf_op jit(solution)/shard_map/pallas_call | solution.py:513
  55.5 0.0 copy-start
  55.5 1.6 %fusion = (bf16[128,256]{1,0:T(8,128)(2,1)}, bf16[128,256]{1,0:T(8,128)(2,1)}, bf16[128,256]{1,0:T(8,128)(2,1)}) fusion(bf16[128,768]{1,0:T(8,128)(2,1)} %get-tuple-element.6), kind=kLoop, calls=%fused_computation | loop fusion | bytes 393216 | tf_op jit(solution)/shard_map/slice | solution.py:584
  57.1 0.0 copy-done
  57.1 0.6 %copy.12 = f32[256,32]{0,1:T(8,128)} copy(f32[256,32]{0,1:T(8,128)S(1)} %bitcast.4) | data formatting | bytes 65536
Async XLA Ops:
  55.5 1.6 %copy-start = (f32[32,256]{1,0:T(8,128)S(1)}, f32[32,256]{1,0:T(8,128)}, u32[]{:S(2)}) copy-start(f32[32,256]{1,0:T(8,128)} %get-tuple-element.7) | copy-start | bytes 98308

commit v5 on v4

--- a/solution.py
+++ b/solution.py
@@ -326,7 +326,7 @@
     stats[y, 0] = own_top
     stats[y, 1] = jnp.sum(shares * lst[...], axis=0)
     stats[y, 2] = jnp.sum(shares * dst[...], axis=0)
-    for k in range(1, ny):
+    for k in sorted(range(1, ny), key=lambda k: -min(k, ny - k)):
         send(stats.at[y], stats.at[y], st_r.at[ny - k], ypeer[k])
 
     cst[...] = shares
@@ -457,11 +457,12 @@
     for d in range(half - 2, 0, -1):
         backward(right_slot(d))
         backward(left_slot(d))
-    query_part()
     for step in range(2, half + 1):
         if step == max(half, 3):
             weight_part()
         reduce_rest(step)
+        if step == 2:
+            query_part()
     if half == 2:
         weight_part()
 

time: 57.9 us -> 57.8 us (level)
  no operation moved by 1% of the time
where the time goes in v5:
time: 57.8 us; the launch traced here: 57.6 us
  Pallas kernels  54.8 us (95%)
  local copies, waits for them, and re-layouts  2.2 us (4%)
  between operations  0.65 us (1%)
    pallas_call x1, Pallas kernels, shards(): pl.pallas_call(functools.partial(kernel, ny, nz), out_shape=(jax.ShapeDty...  54.8 us
    slice x1, local copies, waits for them, and re-layouts, shards(): return (o[:, :B], o[:, B:2 * B], o[:, 2 * B:], jnp.transpose(g))  1.59 us

profile of v5, /device:TPU:4, one launch (start us, length us, event | category | flops | bytes accessed | tf_op | source)
XLA Modules:
  0.0 57.6 jit_solution(15399337910103848550)
XLA Ops:
  0.6 54.8 %shard_map.102 = (bf16[128,768]{1,0:T(8,128)(2,1)}, f32[32,256]{1,0:T(8,128)}) custom-call(bf16[128,256]{1,0:T(8,128)(2,1)} %q_hbm.1, bf16[128,256]{1,0:T(8,128)(2,1)} %k_hbm.1, bf16[128,256]{1,0:T(8,128)(2,1)} %v_hbm.1, bf16[128,2048]{1,0:T(8,128)(2,1)} %og_hbm.1, bf16[256,2048]{1,0:T(8,128)(2,1)} %w_hbm.1, s32[64,128]{1,0:T(8,128)} %bitcast.3, ...), custom_call_target="tpu_custom_call" | custom-call | tf_op jit(solution)/shard_map/pallas_call | solution.py:514
  55.4 0.0 copy-start
  55.4 1.6 %fusion = (bf16[128,256]{1,0:T(8,128)(2,1)}, bf16[128,256]{1,0:T(8,128)(2,1)}, bf16[128,256]{1,0:T(8,128)(2,1)}) fusion(bf16[128,768]{1,0:T(8,128)(2,1)} %get-tuple-element.6), kind=kLoop, calls=%fused_computation | loop fusion | bytes 393216 | tf_op jit(solution)/shard_map/slice | solution.py:585
  57.0 0.0 copy-done
  57.0 0.6 %copy.12 = f32[256,32]{0,1:T(8,128)} copy(f32[256,32]{0,1:T(8,128)S(1)} %bitcast.4) | data formatting | bytes 65536
Async XLA Ops:
  55.4 1.6 %copy-start = (f32[32,256]{1,0:T(8,128)S(1)}, f32[32,256]{1,0:T(8,128)}, u32[]{:S(2)}) copy-start(f32[32,256]{1,0:T(8,128)} %get-tuple-element.7) | copy-start | bytes 98308

commit v6 on v5

--- a/solution.py
+++ b/solution.py
@@ -331,7 +331,7 @@
 
     cst[...] = shares
 
-    for k in [*range(1, ny), 0]:
+    for k in sorted(range(ny), key=lambda k: -min(k, ny - k)):
         b = ypos[k]
         part = jnp.zeros((HD, B), F32)
         for slot in range(nz):
@@ -443,7 +443,7 @@
                 for c in range(2):
                     part += dot(att[h, b, :, pl.ds(c * T, T)], ogb[b, h ^ c])
             gsend[:, :, pl.ds(h * HD, HD)] = jnp.transpose(part).reshape(nz, zcols, HD)
-        for k in range(1, nz):
+        for k in sorted(range(1, nz), key=lambda k: -min(k, nz - k)):
             send(gsend.at[zpos[k]], grecv.at[nz - k], g_r.at[nz - k], zpeer[k])
 
     backward(nz - 1)

time: 57.8 us -> 58.5 us (1.012)
  no operation moved by 1% of the time
where the time goes in v6:
time: 58.5 us; the launch traced here: 57.9 us
  Pallas kernels  55 us (94%)
  local copies, waits for them, and re-layouts  2.2 us (4%)
  between operations  0.65 us (1%)
    pallas_call x1, Pallas kernels, shards(): pl.pallas_call(functools.partial(kernel, ny, nz), out_shape=(jax.ShapeDty...  55 us
    slice x1, local copies, waits for them, and re-layouts, shards(): return (o[:, :B], o[:, B:2 * B], o[:, 2 * B:], jnp.transpose(g))  1.59 us

profile of v6, /device:TPU:4, one launch (start us, length us, event | category | flops | bytes accessed | tf_op | source)
XLA Modules:
  0.0 57.9 jit_solution(9010177735349750131)
XLA Ops:
  0.6 55.0 %shard_map.102 = (bf16[128,768]{1,0:T(8,128)(2,1)}, f32[32,256]{1,0:T(8,128)}) custom-call(bf16[128,256]{1,0:T(8,128)(2,1)} %q_hbm.1, bf16[128,256]{1,0:T(8,128)(2,1)} %k_hbm.1, bf16[128,256]{1,0:T(8,128)(2,1)} %v_hbm.1, bf16[128,2048]{1,0:T(8,128)(2,1)} %og_hbm.1, bf16[256,2048]{1,0:T(8,128)(2,1)} %w_hbm.1, s32[64,128]{1,0:T(8,128)} %bitcast.3, ...), custom_call_target="tpu_custom_call" | custom-call | tf_op jit(solution)/shard_map/pallas_call | solution.py:514
  55.7 0.0 copy-start
  55.7 1.6 %fusion = (bf16[128,256]{1,0:T(8,128)(2,1)}, bf16[128,256]{1,0:T(8,128)(2,1)}, bf16[128,256]{1,0:T(8,128)(2,1)}) fusion(bf16[128,768]{1,0:T(8,128)(2,1)} %get-tuple-element.6), kind=kLoop, calls=%fused_computation | loop fusion | bytes 393216 | tf_op jit(solution)/shard_map/slice | solution.py:585
  57.3 0.0 copy-done
  57.3 0.6 %copy.12 = f32[256,32]{0,1:T(8,128)} copy(f32[256,32]{0,1:T(8,128)S(1)} %bitcast.4) | data formatting | bytes 65536
Async XLA Ops:
  55.7 1.6 %copy-start = (f32[32,256]{1,0:T(8,128)S(1)}, f32[32,256]{1,0:T(8,128)}, u32[]{:S(2)}) copy-start(f32[32,256]{1,0:T(8,128)} %get-tuple-element.7) | copy-start | bytes 98308
